TPU v7x, 128 devices: a whole 4x4x4 slice. The times are simulated.
128 devices in a mesh: grp: 2 (over core), dev: 64 (over y, z, x).
Axes of the slice: x: 4, y: 4, z: 4, core: 2. Of those that a mesh axis runs over, the one named last changes fastest.
Arguments:
- hidden_state: bfloat16 [3, 256, 7168], P(None, ('grp', 'dev')), may hold values from -180 to 180
- ffn_gain: bfloat16 [7168], replicated, may hold values from 0.5 to 1.5
- expert_ids: int32 [3, 256, 8], P(None, ('grp', 'dev')), may hold values from 0 to 15, all different within a row; in each aligned block of 256 rows (0 to 255, 256 to 511, ..., all dimensions but the last counted through in order) at most 192 rows name the same one
- expert_gates: bfloat16 [3, 256, 8], P(None, ('grp', 'dev')), may hold values from 0.049804688 to 0.796875
- w_gate: bfloat16 [7168, 32768], P(None, ('grp', 'dev')), may hold values from -0.0625 to 0.0625
- w_up: bfloat16 [7168, 32768], P(None, ('grp', 'dev')), may hold values from -0.0625 to 0.0625
- w_down: bfloat16 [32768, 7168], P(('grp', 'dev')), may hold values from -0.125 to 0.125
- queries: bfloat16 [3, 256, 128, 576], P(None, ('grp', 'dev')), may hold values from -36 to 36
- kv_cache: bfloat16 [256, 2048, 576], P(('grp', 'dev')), may hold values from -6 to 6
- new_keys: bfloat16 [3, 256, 576], P(None, ('grp', 'dev')), may hold values from -6 to 6
- cache_lengths: int32 [256], P(('grp', 'dev')), may hold values from 256 to 2048, as said below
Outputs:
- attended: bfloat16 [3, 256, 128, 512], P(None, ('grp', 'dev'))
- routed: bfloat16 [3, 256, 7168], P(None, ('grp', 'dev'))
Inputs may be any that keep to these rules, and one draw needn't show every extreme that they name: `expert_ids`: in each step no expert is picked by more than 192 of the 256 tokens; some expert is picked by exactly 192 tokens in some step. `cache_lengths`: some request has all 2048 slots filled.
All inputs are finite; a program needn't handle non-finite values.
Results may differ from a plain program's by a relative error of at most 0.0065.
Values may be sent and summed in bfloat16 or wider, within the bound.
No kernel may reach another device: no remote copies, remote signals or barrier semaphores. Data moves between devices by JAX's collectives and lax.ppermute only.
A program may use at most 192 MiB of HBM per device.

v0:
```python
import functools
import math

import jax
import jax.numpy as jnp
from jax import lax
from jax.experimental import pallas as pl
from jax.experimental.pallas import tpu as pltpu
from jax.sharding import Mesh
from jax.sharding import PartitionSpec as P

KV_RANK = 512
EPS = 1e-06
SCORE_SCALE = 1.0 / math.sqrt(192.0)
AXES = ("c", "y", "z", "x")
SIDE = 4
GATE_LANES = 128
SLOT_CHUNK = 512
FEATURE_CHUNK = 1792
SMALL_VMEM = 4 * 1024 * 1024
ATTEND_VMEM = 16 * 1024 * 1024
JOIN_VMEM = 12 * 1024 * 1024
EXPERT_VMEM = 12 * 1024 * 1024


def device_number(c, y, z, x):
    return ((c * SIDE + y) * SIDE + z) * SIDE + x


def shifted_pairs(axis_of_core, distance):
    pairs = []
    for c in range(2):
        for y in range(SIDE):
            for z in range(SIDE):
                for x in range(SIDE):
                    place = {"y": y, "z": z, "x": x}
                    axis = axis_of_core[c]
                    place[axis] = (place[axis] + distance) % SIDE
                    pairs.append((device_number(c, y, z, x), device_number(c, **place)))
    return pairs


def shift(block, axis_of_core, distance):
    return lax.ppermute(block, AXES, shifted_pairs(axis_of_core, distance))


def other_core(block):
    return lax.ppermute(block, "c", [(0, 1), (1, 0)])


def collect(block, axis_of_core):
    return [
        block,
        shift(block, axis_of_core, -1),
        shift(block, axis_of_core, 1),
        shift(block, axis_of_core, 2),
    ]


def send_home(blocks, axis_of_core):
    return [
        blocks[0],
        shift(blocks[1], axis_of_core, 1),
        shift(blocks[2], axis_of_core, -1),
        shift(blocks[3], axis_of_core, 2),
    ]


def add_up(blocks):
    total = blocks[0].astype(jnp.float32)
    for block in blocks[1:]:
        total = total + block.astype(jnp.float32)
    return total.astype(jnp.bfloat16)


def cut(rows, parts):
    size = rows.shape[0] // parts
    return [rows[i * size : (i + 1) * size] for i in range(parts)]


def prepare_body(state_in, gain_in, id_in, gate_in, out_ref, state_ref, gain_ref, id_ref, gate_ref, sems):
    pairs = ((state_in, state_ref), (gain_in, gain_ref), (id_in, id_ref), (gate_in, gate_ref))
    copies = [pltpu.make_async_copy(a, b, sems.at[i]) for i, (a, b) in enumerate(pairs)]
    for copy in copies:
        copy.start()
    for copy in copies:
        copy.wait()
    steps, requests, features = state_ref.shape
    gain = gain_ref[...].astype(jnp.float32)
    lanes = lax.broadcasted_iota(jnp.int32, (requests, GATE_LANES), 1)
    for s in range(steps):
        rows = pl.ds(s * requests, requests)
        values = state_ref[s].astype(jnp.float32)
        factor = lax.rsqrt(jnp.mean(values * values, axis=-1, keepdims=True) + EPS)
        for j in range(gain.shape[0]):
            at = slice(j * GATE_LANES, (j + 1) * GATE_LANES)
            scaled = values[:, at] * factor * gain[j : j + 1]
            out_ref[rows, at] = scaled.astype(jnp.bfloat16)
        ids, gates = id_ref[s], gate_ref[s].astype(jnp.float32)
        table = jnp.zeros((requests, GATE_LANES), jnp.float32)
        for k in range(ids.shape[1]):
            table = table + jnp.where(lanes == ids[:, k : k + 1], gates[:, k : k + 1], 0.0)
        out_ref[rows, features:] = table.astype(jnp.bfloat16)


def prepare(hidden_state, ffn_gain, expert_ids, expert_gates):
    steps, requests, features = hidden_state.shape
    inputs = (hidden_state, ffn_gain.reshape(-1, GATE_LANES), expert_ids, expert_gates)
    inputs = [in_hbm(a) for a in inputs]
    return pl.pallas_call(
        prepare_body,
        out_shape=jax.ShapeDtypeStruct((steps * requests, features + GATE_LANES), jnp.bfloat16),
        in_specs=[pl.BlockSpec(memory_space=pltpu.HBM)] * len(inputs),
        scratch_shapes=[pltpu.VMEM(a.shape, a.dtype) for a in inputs]
        + [pltpu.SemaphoreType.DMA((len(inputs),))],
        compiler_params=pltpu.CompilerParams(vmem_limit_bytes=SMALL_VMEM),
        name="prepare",
    )(*inputs)


def in_hbm(array):
    return pltpu.with_memory_space_constraint(array, pltpu.HBM)


def stack_body(*refs):
    rows = refs[0].shape[0]
    for i, ref in enumerate(refs[:-1]):
        refs[-1][pl.ds(i * rows, rows), :] = ref[...]


def stack(blocks):
    if len(blocks) == 1:
        return blocks[0]
    rows, width = blocks[0].shape
    return pl.pallas_call(
        stack_body,
        out_shape=jax.ShapeDtypeStruct((rows * len(blocks), width), blocks[0].dtype),
        compiler_params=pltpu.CompilerParams(vmem_limit_bytes=SMALL_VMEM),
        name="stack",
    )(*blocks)


def attend_body(length_ref, q_ref, k_ref, fresh_ref, out_ref, score_ref):
    request = pl.program_id(0)
    length = length_ref[request]
    steps, heads = q_ref.shape[0], q_ref.shape[3]
    slots = k_ref.shape[2]
    q = jnp.concatenate([q_ref[s, 0].T for s in range(steps)], axis=0)
    fresh = fresh_ref[0]
    fresh_scores = (
        lax.dot_general(q, fresh, (((1,), (1,)), ((), ())), preferred_element_type=jnp.float32)
        * SCORE_SCALE
    )
    row_step = lax.broadcasted_iota(jnp.int32, fresh_scores.shape, 0) // heads
    fresh_lane = lax.broadcasted_iota(jnp.int32, fresh_scores.shape, 1)
    fresh_scores = jnp.where(fresh_lane <= row_step, fresh_scores, -jnp.inf)
    top = jnp.max(fresh_scores, axis=1, keepdims=True)
    for start in range(0, slots, SLOT_CHUNK):
        cols = pl.ds(start, SLOT_CHUNK)
        scores = jnp.dot(q, k_ref[0, :, cols], preferred_element_type=jnp.float32) * SCORE_SCALE
        slot = lax.broadcasted_iota(jnp.int32, scores.shape, 1) + start
        scores = jnp.where(slot < length, scores, -jnp.inf)
        score_ref[:, cols] = scores
        top = jnp.maximum(top, jnp.max(scores, axis=1, keepdims=True))
    fresh_exp = jnp.exp(fresh_scores - top)
    denominator = jnp.sum(fresh_exp, axis=1, keepdims=True)
    total = jnp.dot(
        fresh_exp.astype(jnp.bfloat16), fresh[:, :KV_RANK], preferred_element_type=jnp.float32
    )
    for start in range(0, slots, SLOT_CHUNK):
        cols = pl.ds(start, SLOT_CHUNK)
        weights = jnp.exp(score_ref[:, cols] - top)
        denominator = denominator + jnp.sum(weights, axis=1, keepdims=True)
        total = total + lax.dot_general(
            weights.astype(jnp.bfloat16),
            k_ref[0, :KV_RANK, cols],
            (((1,), (1,)), ((), ())),
            preferred_element_type=jnp.float32,
        )
    result = (total / denominator).astype(jnp.bfloat16)
    for s in range(steps):
        out_ref[s, 0] = result[s * heads : (s + 1) * heads]


def attend(queries, kv_cache, new_keys, cache_lengths):
    steps, requests, heads, width = queries.shape
    slots = kv_cache.shape[1]
    q_t = jnp.swapaxes(queries, 2, 3)
    k_t = jnp.swapaxes(kv_cache, 1, 2)
    fresh = jnp.pad(jnp.swapaxes(new_keys, 0, 1), ((0, 0), (0, 16 - steps), (0, 0)))
    return pl.pallas_call(
        attend_body,
        out_shape=jax.ShapeDtypeStruct((steps, requests, heads, KV_RANK), jnp.bfloat16),
        grid=(requests,),
        in_specs=[
            pl.BlockSpec(memory_space=pltpu.SMEM),
            pl.BlockSpec((steps, 1, width, heads), lambda r: (0, r, 0, 0)),
            pl.BlockSpec((1, width, slots), lambda r: (r, 0, 0)),
            pl.BlockSpec((1, 16, width), lambda r: (r, 0, 0)),
        ],
        out_specs=pl.BlockSpec((steps, 1, heads, KV_RANK), lambda r: (0, r, 0, 0)),
        scratch_shapes=[pltpu.VMEM((steps * heads, slots), jnp.float32)],
        compiler_params=pltpu.CompilerParams(vmem_limit_bytes=ATTEND_VMEM),
        cost_estimate=pl.CostEstimate(
            flops=2 * steps * requests * heads * slots * (width + KV_RANK),
            bytes_accessed=2 * requests * (slots * width + steps * heads * (width + KV_RANK)),
            transcendentals=steps * requests * heads * slots,
        ),
        name="attend",
    )(cache_lengths, in_hbm(q_t), in_hbm(k_t), fresh)


def join_body(*refs):
    in_refs, out_refs = refs[:-SIDE], refs[-SIDE:]
    half = len(in_refs) // 2
    mine, back = (
        jnp.concatenate([r[...].astype(jnp.float32) for r in part], axis=0)
        for part in (in_refs[:half], in_refs[half:])
    )
    total = (mine + back).astype(jnp.bfloat16)
    for out_ref, piece in zip(out_refs, cut(total, SIDE)):
        out_ref[...] = piece


def join(mine, back):
    rows, width = sum(b.shape[0] for b in back), back[0].shape[1]
    piece = jax.ShapeDtypeStruct((rows // SIDE, width), back[0].dtype)
    return pl.pallas_call(
        join_body,
        out_shape=[piece] * SIDE,
        compiler_params=pltpu.CompilerParams(vmem_limit_bytes=JOIN_VMEM),
        name="join",
    )(*mine, *back)


def hold_body(*refs):
    pass


def hold(blocks, after):
    anywhere = pl.BlockSpec(memory_space=pl.ANY)
    return pl.pallas_call(
        hold_body,
        out_shape=[jax.ShapeDtypeStruct(b.shape, b.dtype) for b in blocks],
        in_specs=[anywhere] * (len(blocks) + len(after)),
        out_specs=[anywhere] * len(blocks),
        input_output_aliases={i: i for i in range(len(blocks))},
        compiler_params=pltpu.CompilerParams(vmem_limit_bytes=1024 * 1024),
        name="hold",
    )(*blocks, *after)


def resident_body(*refs, count):
    sems, outs = refs[-1], refs[-1 - count : -1]
    copies = [pltpu.make_async_copy(refs[i], outs[i], sems.at[i]) for i in range(count)]
    for copy in copies:
        copy.start()
    for copy in copies:
        copy.wait()


def resident(weights, after):
    count = len(weights)
    return pl.pallas_call(
        functools.partial(resident_body, count=count),
        out_shape=[pltpu.VMEM(w.shape, w.dtype) for w in weights],
        in_specs=[pl.BlockSpec(memory_space=pltpu.HBM)] * count
        + [pl.BlockSpec(memory_space=pl.ANY)] * len(after),
        out_specs=[pl.BlockSpec(memory_space=pltpu.VMEM)] * count,
        scratch_shapes=[pltpu.SemaphoreType.DMA((count,))],
        compiler_params=pltpu.CompilerParams(vmem_limit_bytes=SMALL_VMEM),
        name="resident",
    )(*[in_hbm(w) for w in weights], *after)


def expert_body(*refs, count):
    token_refs = refs[:count]
    gate_w, up_w, down_w = refs[count : count + 3]
    out_refs = refs[-count:]
    features = gate_w.shape[0]
    heights = [r.shape[0] for r in token_refs]

    def tokens(at):
        return jnp.concatenate([r[:, at] for r in token_refs], axis=0)

    gates = tokens(pl.ds(features, GATE_LANES)).astype(jnp.float32)
    core, y, z = (lax.axis_index(name) for name in ("c", "y", "z"))
    expert = (core * SIDE + y) * 2 + (z >= SIDE // 2).astype(jnp.int32)
    lanes = lax.broadcasted_iota(jnp.int32, gates.shape, 1)
    column = jnp.sum(jnp.where(lanes == expert, gates, 0.0), axis=1, keepdims=True)

    chunks = [pl.ds(i, FEATURE_CHUNK) for i in range(0, features, FEATURE_CHUNK)]
    gate = up = None
    for at in chunks:
        rows = tokens(at)
        more_gate = jnp.dot(rows, gate_w[at, :], preferred_element_type=jnp.float32)
        more_up = jnp.dot(rows, up_w[at, :], preferred_element_type=jnp.float32)
        gate = more_gate if gate is None else gate + more_gate
        up = more_up if up is None else up + more_up
    hidden = (gate / (1.0 + jnp.exp(-gate)) * up).astype(jnp.bfloat16)
    for at in chunks:
        outs = jnp.dot(hidden, down_w[:, at], preferred_element_type=jnp.float32)
        outs = (outs * column).astype(jnp.bfloat16)
        top = 0
        for out_ref, height in zip(out_refs, heights):
            out_ref[:, at] = outs[top : top + height]
            top += height


def expert_call(blocks, weights, after):
    count = len(blocks)
    heights = [b.shape[0] for b in blocks]
    all_rows = sum(heights)
    features, hidden_units = weights[0].shape
    whole = pl.BlockSpec(memory_space=pltpu.VMEM)
    return pl.pallas_call(
        functools.partial(expert_body, count=count),
        out_shape=[jax.ShapeDtypeStruct((h, features), jnp.bfloat16) for h in heights],
        in_specs=[whole] * (count + 3) + [pl.BlockSpec(memory_space=pl.ANY)] * len(after),
        out_specs=[whole] * count,
        compiler_params=pltpu.CompilerParams(vmem_limit_bytes=EXPERT_VMEM),
        cost_estimate=pl.CostEstimate(
            flops=6 * all_rows * features * hidden_units,
            bytes_accessed=4 * all_rows * features,
            transcendentals=all_rows * hidden_units,
        ),
        name="experts",
    )(*blocks, *weights, *after)


def routed_block(
    hidden_state, ffn_gain, expert_ids, expert_gates, w_gate, w_up, w_down, attended
):
    steps, requests, features = hidden_state.shape
    near, middle, far = ("z", "x"), ("y", "z"), ("x", "y")
    own = prepare(hidden_state, ffn_gain, expert_ids, expert_gates)
    own = stack(collect(own, near))
    pieces = collect(own, middle)
    first, second = stack(pieces[:2]), stack(pieces[2:])

    def apply_expert(blocks, after):
        theirs = other_core(stack(blocks))
        *mine, theirs = expert_call([*blocks, theirs], weights, after)
        return mine, other_core(theirs)

    def merge(mine, received):
        return [add_up(pair) for pair in zip(mine, cut(received, len(mine)))]

    def neighbours(block):
        return [shift(block, far, -1), shift(block, far, 1)]

    arrived = neighbours(first) + neighbours(second)
    weights = resident([w_gate, w_up, w_down], [in_hbm(attended), *arrived[:2]])
    own, *arrived = hold([stack([first, second]), *arrived], weights)
    opposite = [shift(arrived[0], far, -1), shift(arrived[3], far, 1)]
    outs, back = apply_expert(arrived[:2], [])
    sums = merge(outs, back)
    outs, back = apply_expert(arrived[2:], outs[:1])
    sums += merge(outs, back)
    home = [shift(stack(sums[0::2]), far, 1), shift(stack(sums[1::2]), far, -1)]
    own_out, own_back = apply_expert([own], outs[:1])
    opposite = hold(opposite, [*sums, *own_out])
    theirs = [other_core(block) for block in opposite]
    outs = expert_call([*opposite, *theirs], weights, own_out)
    back = [other_core(block) for block in hold(outs[2:], [*home, own_back])]
    own_sum = add_up([own_out[0], own_back])
    far_sum = add_up(send_home(join(outs[:2], back), middle))
    far_sum = shift(far_sum, far, 2)
    blocks = [cut(block, SIDE) for block in (own_sum, *home)]
    summed = send_home([add_up(p) for p in zip(*blocks)], middle)
    summed = add_up([*summed, far_sum])
    summed = add_up(send_home(cut(summed, SIDE), near))
    return summed.reshape(steps, requests, features)


def on_device(
    hidden_state,
    ffn_gain,
    expert_ids,
    expert_gates,
    w_gate,
    w_up,
    w_down,
    queries,
    kv_cache,
    new_keys,
    cache_lengths,
):
    attended = attend(queries, kv_cache, new_keys, cache_lengths)
    routed = routed_block(
        hidden_state, ffn_gain, expert_ids, expert_gates, w_gate, w_up, w_down, attended
    )
    return attended, routed


def solution(mesh):
    chips = Mesh(mesh.devices.reshape(2, SIDE, SIDE, SIDE), AXES)
    placed = (
        P(None, AXES, None),
        P(),
        P(None, AXES, None),
        P(None, AXES, None),
        P(None, AXES),
        P(None, AXES),
        P(AXES, None),
        P(None, AXES, None, None),
        P(AXES, None, None),
        P(None, AXES, None),
        P(AXES),
    )
    return jax.shard_map(
        on_device,
        mesh=chips,
        in_specs=placed,
        out_specs=(P(None, AXES, None, None), P(None, AXES, None)),
        check_vma=False,
    )
```

profile of v0, /device:TPU:0, one launch (start us, length us, event | category | flops | bytes accessed | tf_op | source)
XLA Modules:
  0.0 120.1 jit_solution(5595856641841183315)
XLA Ops:
  0.6 1.2 prepare.1.refs_0_
  1.8 4.2 %collective-permute-start = (bf16[6,7296]{1,0:T(8,128)(2,1)S(1)}, bf16[6,7296]{1,0:T(8,128)(2,1)S(1)}, u32[]{:S(2)}, u32[]{:S(2)}) collective-permute-start(bf16[6,7296]{1,0:T(8,128)(2,1)S(1)} %prepare.1.refs_0_), channel_id=1, source_target_pairs={{0,12},{1,13},{2,14},{3,15},{4,0},{5,1},{6,2},{7,3},{8,4},{9,5},{1... | collective-permute-start | bytes 262664 | tf_op jit(solution)/shard_map/ppermute | solution.py:44
  6.0 1.9 %collective-permute-start.2 = (bf16[6,7296]{1,0:T(8,128)(2,1)S(1)}, bf16[6,7296]{1,0:T(8,128)(2,1)S(1)}, u32[]{:S(2)}, u32[]{:S(2)}) collective-permute-start(bf16[6,7296]{1,0:T(8,128)(2,1)S(1)} %prepare.1.refs_0_), channel_id=1, source_target_pairs={{0,8},{1,9},{2,10},{3,11},{4,12},{5,13},{6,14},{7,15},{8,0},{9,1},... | collective-permute-start | bytes 262664 | tf_op jit(solution)/shard_map/ppermute | solution.py:44
  7.9 0.5 collective-permute-done.refs_1_
  8.4 4.9 %collective-permute-done.1.refs_2_ = bf16[6,7296]{1,0:T(8,128)(2,1)S(1)} collective-permute-done((bf16[6,7296]{1,0:T(8,128)(2,1)S(1)}, bf16[6,7296]{1,0:T(8,128)(2,1)S(1)}, u32[]{:S(2)}, u32[]{:S(2)}) %collective-permute-start.1) | collective-permute-done | bytes 87584 | tf_op jit(solution)/shard_map/ppermute | solution.py:44
  13.4 3.1 %collective-permute-start.3 = (bf16[24,7296]{1,0:T(8,128)(2,1)S(1)}, bf16[24,7296]{1,0:T(8,128)(2,1)S(1)}, u32[]{:S(2)}, u32[]{:S(2)}) collective-permute-start(bf16[24,7296]{1,0:T(8,128)(2,1)S(1)} %stack.8.refs_0_), channel_id=1, source_target_pairs={{0,48},{1,49},{2,50},{3,51},{4,52},{5,53},{6,54},{7,55},{8,56},{9,... | collective-permute-start | bytes 1050632 | tf_op jit(solution)/shard_map/ppermute | solution.py:44
  16.5 2.2 %collective-permute-start.5 = (bf16[24,7296]{1,0:T(8,128)(2,1)S(1)}, bf16[24,7296]{1,0:T(8,128)(2,1)S(1)}, u32[]{:S(2)}, u32[]{:S(2)}) collective-permute-start(bf16[24,7296]{1,0:T(8,128)(2,1)S(1)} %stack.8.refs_0_), channel_id=1, source_target_pairs={{0,32},{1,33},{2,34},{3,35},{4,36},{5,37},{6,38},{7,39},{8,40},{9,... | collective-permute-start | bytes 1050632 | tf_op jit(solution)/shard_map/ppermute | solution.py:44
  18.7 2.7 %collective-permute-done.3.refs_1_ = bf16[24,7296]{1,0:T(8,128)(2,1)S(1)} collective-permute-done((bf16[24,7296]{1,0:T(8,128)(2,1)S(1)}, bf16[24,7296]{1,0:T(8,128)(2,1)S(1)}, u32[]{:S(2)}, u32[]{:S(2)}) %collective-permute-start.3) | collective-permute-done | bytes 350240 | tf_op jit(solution)/shard_map/ppermute | solution.py:44
  21.4 2.8 %collective-permute-start.6 = (bf16[48,7296]{1,0:T(8,128)(2,1)S(1)}, bf16[48,7296]{1,0:T(8,128)(2,1)S(1)}, u32[]{:S(2)}, u32[]{:S(2)}) collective-permute-start(bf16[48,7296]{1,0:T(8,128)(2,1)S(1)} %stack.9.refs_0_), channel_id=1, source_target_pairs={{0,3},{1,0},{2,1},{3,2},{4,7},{5,4},{6,5},{7,6},{8,11},{9,8},{10,9... | collective-permute-start | bytes 2101256 | tf_op jit(solution)/shard_map/ppermute | solution.py:44
  24.2 4.5 %collective-permute-done.4.refs_0_ = bf16[24,7296]{1,0:T(8,128)(2,1)S(1)} collective-permute-done((bf16[24,7296]{1,0:T(8,128)(2,1)S(1)}, bf16[24,7296]{1,0:T(8,128)(2,1)S(1)}, u32[]{:S(2)}, u32[]{:S(2)}) %collective-permute-start.4) | collective-permute-done | bytes 350240 | tf_op jit(solution)/shard_map/ppermute | solution.py:44
  28.8 3.3 %collective-permute-start.8 = (bf16[48,7296]{1,0:T(8,128)(2,1)S(1)}, bf16[48,7296]{1,0:T(8,128)(2,1)S(1)}, u32[]{:S(2)}, u32[]{:S(2)}) collective-permute-start(bf16[48,7296]{1,0:T(8,128)(2,1)S(1)} %stack.10.refs_1_), channel_id=1, source_target_pairs={{0,3},{1,0},{2,1},{3,2},{4,7},{5,4},{6,5},{7,6},{8,11},{9,8},{10,9... | collective-permute-start | bytes 2101256 | tf_op jit(solution)/shard_map/ppermute | solution.py:44
  32.1 8.3 %attend.1.refs_3_ = bf16[3,2,128,512]{3,2,1,0:T(8,128)(2,1)} custom-call(s32[2]{0:T(128)S(1)} %copy-done, bf16[3,2,576,128]{3,2,1,0:T(8,128)(2,1)} %bitcast.9, bf16[2,576,2048]{2,1,0:T(8,128)(2,1)} %bitcast.8, bf16[2,16,576]{2,1,0:T(8,128)(2,1)S(1)} %pad.4.fresh_ref), custom_call_target="tpu_custom_call" | custom-call | flops 3422552064 | bytes 6389760 | tf_op jit(solution)/shard_map/attend/pallas_call | solution.py:191
  40.4 0.1 stack.11.refs_0_
  40.5 4.2 %resident.1 = (bf16[7168,256]{1,0:T(8,128)(2,1)S(1)}, bf16[7168,256]{1,0:T(8,128)(2,1)S(1)}, bf16[256,7168]{1,0:T(8,128)(2,1)S(1)}) custom-call(bf16[7168,256]{1,0:T(8,128)(2,1)} %refs_0_.1, bf16[7168,256]{1,0:T(8,128)(2,1)} %refs_1_.1, bf16[256,7168]{1,0:T(8,128)(2,1)} %refs_2_.1, bf16[3,2,128,512]{3,2,1,0:T(8,128)(2,1)} %attend.1.refs_3_, ...), custom_call_target="tpu_custom_call" | custom-call | tf_op jit(solution)/shard_map/resident/pallas_call | solution.py:264
  44.8 0.1 stack.13
  44.9 0.1 collective-permute-start.12
  45.0 0.1 stack.12
  45.1 0.6 collective-permute-start.11
  45.6 0.1 collective-permute-start.10
  45.7 2.4 %collective-permute-done.12.refs_2_ = bf16[96,7296]{1,0:T(8,128)(2,1)S(1)} collective-permute-done((bf16[96,7296]{1,0:T(8,128)(2,1)S(1)}, bf16[96,7296]{1,0:T(8,128)(2,1)S(1)}, u32[]{:S(2)}, u32[]{:S(2)}) %collective-permute-start.12) | collective-permute-done | bytes 1400864 | tf_op jit(solution)/shard_map/ppermute | solution.py:48
  48.1 2.4 %experts.4 = (bf16[48,7168]{1,0:T(8,128)(2,1)S(1)}, bf16[48,7168]{1,0:T(8,128)(2,1)S(1)}, bf16[96,7168]{1,0:T(8,128)(2,1)S(1)}) custom-call(bf16[48,7296]{1,0:T(8,128)(2,1)S(1)} %get-tuple-element.36.refs_0_, bf16[48,7296]{1,0:T(8,128)(2,1)S(1)} %get-tuple-element.37.refs_1_, bf16[96,7296]{1,0:T(8,128)(2,1)S(1)} %collective-permute-done.12.refs_2_, ...), custom_call_target="tpu_custom_call" | custom-call | flops 2113929216 | bytes 5505024 | tf_op jit(solution)/shard_map/experts/pallas_call | solution.py:316
  50.6 0.2 collective-permute-start.14
  50.8 3.2 %collective-permute-start.21 = (bf16[48,7296]{1,0:T(8,128)(2,1)S(1)}, bf16[48,7296]{1,0:T(8,128)(2,1)S(1)}, u32[]{:S(2)}, u32[]{:S(2)}) collective-permute-start(bf16[48,7296]{1,0:T(8,128)(2,1)S(1)} %get-tuple-element.36.refs_0_), channel_id=1, source_target_pairs={{0,3},{1,0},{2,1},{3,2},{4,7},{5,4},{6,5},{7,6},{8,11},{9,8},{10,9... | collective-permute-start | bytes 2101256 | tf_op jit(solution)/shard_map/ppermute | solution.py:44
  54.0 2.5 %experts.5 = (bf16[48,7168]{1,0:T(8,128)(2,1)S(1)}, bf16[48,7168]{1,0:T(8,128)(2,1)S(1)}, bf16[96,7168]{1,0:T(8,128)(2,1)S(1)}) custom-call(bf16[48,7296]{1,0:T(8,128)(2,1)S(1)} %get-tuple-element.34.refs_0_, bf16[48,7296]{1,0:T(8,128)(2,1)S(1)} %get-tuple-element.35.refs_1_, bf16[96,7296]{1,0:T(8,128)(2,1)S(1)} %collective-permute-done.11.refs_2_, ...), custom_call_target="tpu_custom_call" | custom-call | flops 2113929216 | bytes 5505024 | tf_op jit(solution)/shard_map/experts/pallas_call | solution.py:316
  56.5 2.2 %collective-permute-start.15 = (bf16[96,7168]{1,0:T(8,128)(2,1)S(1)}, bf16[96,7168]{1,0:T(8,128)(2,1)S(1)}, u32[]{:S(2)}, u32[]{:S(2)}) collective-permute-start(bf16[96,7168]{1,0:T(8,128)(2,1)S(1)} %get-tuple-element.43), channel_id=1, source_target_pairs={{0,64},{64,0},{1,65},{65,1},{2,66},{66,2},{3,67},{67,3},{4,68},{68... | collective-permute-start | bytes 4128776 | tf_op jit(solution)/shard_map/ppermute | solution.py:48
  58.7 2.5 %experts.6 = (bf16[96,7168]{1,0:T(8,128)(2,1)S(1)}, bf16[96,7168]{1,0:T(8,128)(2,1)S(1)}) custom-call(bf16[96,7296]{1,0:T(8,128)(2,1)S(1)} %get-tuple-element.33.refs_0_, bf16[96,7296]{1,0:T(8,128)(2,1)S(1)} %collective-permute-done.10.refs_1_, bf16[7168,256]{1,0:T(8,128)(2,1)S(1)} %get-tuple-element.30.refs_5_.refs_3_.refs_2_.refs_4_, ...), custom_call_target="tpu_custom_call" | custom-call | flops 2113929216 | bytes 5505024 | tf_op jit(solution)/shard_map/experts/pallas_call | solution.py:316
  61.2 0.1 collective-permute-start.13
  61.3 0.3 add_convert_fusion.2
  61.6 0.3 add_convert_fusion.1
  62.0 0.1 stack.14
  62.2 0.1 stack.15
  62.3 3.3 %collective-permute-start.17 = (bf16[96,7168]{1,0:T(8,128)(2,1)S(1)}, bf16[96,7168]{1,0:T(8,128)(2,1)S(1)}, u32[]{:S(2)}, u32[]{:S(2)}) collective-permute-start(bf16[96,7168]{1,0:T(8,128)(2,1)S(1)} %stack.15), channel_id=1, source_target_pairs={{0,3},{1,0},{2,1},{3,2},{4,7},{5,4},{6,5},{7,6},{8,11},{9,8},{10,9... | collective-permute-start | bytes 4128776 | tf_op jit(solution)/shard_map/ppermute | solution.py:44
  65.6 0.7 collective-permute-done.22.refs_1_
  66.3 1.3 %collective-permute-start.23 = (bf16[48,7296]{1,0:T(8,128)(2,1)S(1)}, bf16[48,7296]{1,0:T(8,128)(2,1)S(1)}, u32[]{:S(2)}, u32[]{:S(2)}) collective-permute-start(bf16[48,7296]{1,0:T(8,128)(2,1)S(1)} %get-tuple-element.46.refs_0_), channel_id=1, source_target_pairs={{0,64},{64,0},{1,65},{65,1},{2,66},{66,2},{3,67},{67,3},{4,68},{68... | collective-permute-start | bytes 2101256 | tf_op jit(solution)/shard_map/ppermute | solution.py:48
  67.6 1.8 %collective-permute-done.23.refs_2_ = bf16[48,7296]{1,0:T(8,128)(2,1)S(1)} collective-permute-done((bf16[48,7296]{1,0:T(8,128)(2,1)S(1)}, bf16[48,7296]{1,0:T(8,128)(2,1)S(1)}, u32[]{:S(2)}, u32[]{:S(2)}) %collective-permute-start.23) | collective-permute-done | bytes 700448 | tf_op jit(solution)/shard_map/ppermute | solution.py:48
  69.4 1.0 collective-permute-done.24.refs_3_
  70.4 2.5 %experts.7 = (bf16[48,7168]{1,0:T(8,128)(2,1)S(1)}, bf16[48,7168]{1,0:T(8,128)(2,1)S(1)}, bf16[48,7168]{1,0:T(8,128)(2,1)S(1)}, bf16[48,7168]{1,0:T(8,128)(2,1)S(1)}) custom-call(bf16[48,7296]{1,0:T(8,128)(2,1)S(1)} %get-tuple-element.46.refs_0_, bf16[48,7296]{1,0:T(8,128)(2,1)S(1)} %get-tuple-element.47.refs_1_, ...), custom_call_target="tpu_custom_call" | custom-call | flops 2113929216 | bytes 5505024 | tf_op jit(solution)/shard_map/experts/pallas_call | solution.py:316
  72.9 8.8 %collective-permute-done.16.refs_2_ = bf16[96,7168]{1,0:T(8,128)(2,1)S(1)} collective-permute-done((bf16[96,7168]{1,0:T(8,128)(2,1)S(1)}, bf16[96,7168]{1,0:T(8,128)(2,1)S(1)}, u32[]{:S(2)}, u32[]{:S(2)}) %collective-permute-start.16) | collective-permute-done | bytes 1376288 | tf_op jit(solution)/shard_map/ppermute | solution.py:44
  81.7 0.4 collective-permute-start.25
  82.0 0.2 collective-permute-start.26
  82.2 0.3 add_convert_fusion
  82.5 1.3 %collective-permute-done.25.refs_2_ = bf16[48,7168]{1,0:T(8,128)(2,1)S(1)} collective-permute-done((bf16[48,7168]{1,0:T(8,128)(2,1)S(1)}, bf16[48,7168]{1,0:T(8,128)(2,1)S(1)}, u32[]{:S(2)}, u32[]{:S(2)}) %collective-permute-start.25) | collective-permute-done | bytes 688160 | tf_op jit(solution)/shard_map/ppermute | solution.py:48
  83.8 1.0 collective-permute-done.26.refs_3_
  84.8 0.3 join.1
  85.1 2.1 %collective-permute-start.29 = (bf16[24,7168]{1,0:T(8,128)(2,1)S(1)}, bf16[24,7168]{1,0:T(8,128)(2,1)S(1)}, u32[]{:S(2)}, u32[]{:S(2)}) collective-permute-start(bf16[24,7168]{1,0:T(8,128)(2,1)S(1)} %get-tuple-element.57), channel_id=1, source_target_pairs={{0,32},{1,33},{2,34},{3,35},{4,36},{5,37},{6,38},{7,39},{8,40},{9,... | collective-permute-start | bytes 1032200 | tf_op jit(solution)/shard_map/ppermute | solution.py:44
  87.3 1.0 collective-permute-start.28
  88.2 1.0 collective-permute-start.27
  89.3 0.4 add_convert_fusion.9
  89.7 1.9 %collective-permute-start.20 = (bf16[24,7168]{1,0:T(8,128)(2,1)S(1)}, bf16[24,7168]{1,0:T(8,128)(2,1)S(1)}, u32[]{:S(2)}, u32[]{:S(2)}) collective-permute-start(bf16[24,7168]{1,0:T(8,128)(2,1)S(1)} %get-tuple-element.59), channel_id=1, source_target_pairs={{0,32},{1,33},{2,34},{3,35},{4,36},{5,37},{6,38},{7,39},{8,40},{9,... | collective-permute-start | bytes 1032200 | tf_op jit(solution)/shard_map/ppermute | solution.py:44
  91.5 2.6 %collective-permute-start.19 = (bf16[24,7168]{1,0:T(8,128)(2,1)S(1)}, bf16[24,7168]{1,0:T(8,128)(2,1)S(1)}, u32[]{:S(2)}, u32[]{:S(2)}) collective-permute-start(bf16[24,7168]{1,0:T(8,128)(2,1)S(1)} %get-tuple-element.60), channel_id=1, source_target_pairs={{0,48},{1,49},{2,50},{3,51},{4,52},{5,53},{6,54},{7,55},{8,56},{9,... | collective-permute-start | bytes 1032200 | tf_op jit(solution)/shard_map/ppermute | solution.py:44
  94.2 0.2 collective-permute-start.18
  94.4 3.6 %collective-permute-done.28 = bf16[24,7168]{1,0:T(8,128)(2,1)S(1)} collective-permute-done((bf16[24,7168]{1,0:T(8,128)(2,1)S(1)}, bf16[24,7168]{1,0:T(8,128)(2,1)S(1)}, u32[]{:S(2)}, u32[]{:S(2)}) %collective-permute-start.28) | collective-permute-done | bytes 344096 | tf_op jit(solution)/shard_map/ppermute | solution.py:44
  98.0 0.2 add_convert_fusion.6
  98.2 1.7 %collective-permute-start.30 = (bf16[24,7168]{1,0:T(8,128)(2,1)S(1)}, bf16[24,7168]{1,0:T(8,128)(2,1)S(1)}, u32[]{:S(2)}, u32[]{:S(2)}) collective-permute-start(bf16[24,7168]{1,0:T(8,128)(2,1)S(1)} %add_convert_fusion.6), channel_id=1, source_target_pairs={{0,2},{1,3},{2,0},{3,1},{4,6},{5,7},{6,4},{7,5},{8,10},{9,11},{10,... | collective-permute-start | bytes 1032200 | tf_op jit(solution)/shard_map/ppermute | solution.py:44
  99.9 1.6 %collective-permute-done.20 = bf16[24,7168]{1,0:T(8,128)(2,1)S(1)} collective-permute-done((bf16[24,7168]{1,0:T(8,128)(2,1)S(1)}, bf16[24,7168]{1,0:T(8,128)(2,1)S(1)}, u32[]{:S(2)}, u32[]{:S(2)}) %collective-permute-start.20) | collective-permute-done | bytes 344096 | tf_op jit(solution)/shard_map/ppermute | solution.py:44
  101.4 6.6 %collective-permute-done.19 = bf16[24,7168]{1,0:T(8,128)(2,1)S(1)} collective-permute-done((bf16[24,7168]{1,0:T(8,128)(2,1)S(1)}, bf16[24,7168]{1,0:T(8,128)(2,1)S(1)}, u32[]{:S(2)}, u32[]{:S(2)}) %collective-permute-start.19) | collective-permute-done | bytes 344096 | tf_op jit(solution)/shard_map/ppermute | solution.py:44
  108.1 0.3 add_convert_fusion.5
  108.5 0.4 collective-permute-start.33
  108.9 4.4 %collective-permute-start.32 = (bf16[6,7168]{1,0:T(8,128)(2,1)S(1)}, bf16[6,7168]{1,0:T(8,128)(2,1)S(1)}, u32[]{:S(2)}, u32[]{:S(2)}) collective-permute-start(bf16[6,7168]{1,0:T(8,128)(2,1)S(1)} %get-tuple-element.67), channel_id=1, source_target_pairs={{0,12},{1,13},{2,14},{3,15},{4,0},{5,1},{6,2},{7,3},{8,4},{9,5},{1... | collective-permute-start | bytes 258056 | tf_op jit(solution)/shard_map/ppermute | solution.py:44
  113.3 0.8 collective-permute-start.31
  114.1 0.8 collective-permute-done.33
  114.9 3.3 %collective-permute-done.32 = bf16[6,7168]{1,0:T(8,128)(2,1)S(1)} collective-permute-done((bf16[6,7168]{1,0:T(8,128)(2,1)S(1)}, bf16[6,7168]{1,0:T(8,128)(2,1)S(1)}, u32[]{:S(2)}, u32[]{:S(2)}) %collective-permute-start.32) | collective-permute-done | bytes 86048 | tf_op jit(solution)/shard_map/ppermute | solution.py:44
  118.2 1.2 collective-permute-done.31
  119.4 0.7 reshape.11
  (38 shorter events, 0.5 us)
Async XLA Ops:
  1.8 6.6 %collective-permute-start = (bf16[6,7296]{1,0:T(8,128)(2,1)S(1)}, bf16[6,7296]{1,0:T(8,128)(2,1)S(1)}, u32[]{:S(2)}, u32[]{:S(2)}) collective-permute-start(bf16[6,7296]{1,0:T(8,128)(2,1)S(1)} %prepare.1.refs_0_), channel_id=1, source_target_pairs={{0,12},{1,13},{2,14},{3,15},{4,0},{5,1},{6,2},{7,3},{8,4},{9,5},{1... | collective-permute-start | bytes 262664 | tf_op jit(solution)/shard_map/ppermute | solution.py:44
  6.0 7.3 %collective-permute-start.1 = (bf16[6,7296]{1,0:T(8,128)(2,1)S(1)}, bf16[6,7296]{1,0:T(8,128)(2,1)S(1)}, u32[]{:S(2)}, u32[]{:S(2)}) collective-permute-start(bf16[6,7296]{1,0:T(8,128)(2,1)S(1)} %prepare.1.refs_0_), channel_id=1, source_target_pairs={{0,4},{1,5},{2,6},{3,7},{4,8},{5,9},{6,10},{7,11},{8,12},{9,13},{1... | collective-permute-start | bytes 262664 | tf_op jit(solution)/shard_map/ppermute | solution.py:44
  6.0 7.3 %collective-permute-start.2 = (bf16[6,7296]{1,0:T(8,128)(2,1)S(1)}, bf16[6,7296]{1,0:T(8,128)(2,1)S(1)}, u32[]{:S(2)}, u32[]{:S(2)}) collective-permute-start(bf16[6,7296]{1,0:T(8,128)(2,1)S(1)} %prepare.1.refs_0_), channel_id=1, source_target_pairs={{0,8},{1,9},{2,10},{3,11},{4,12},{5,13},{6,14},{7,15},{8,0},{9,1},... | collective-permute-start | bytes 262664 | tf_op jit(solution)/shard_map/ppermute | solution.py:44
  13.4 18.7 %copy-start.1 = (bf16[3,2,576]{2,1,0:T(2,128)(2,1)S(1)}, bf16[3,2,576]{2,1,0:T(2,128)(2,1)}, u32[]{:S(2)}) copy-start(bf16[3,2,576]{2,1,0:T(2,128)(2,1)} %param.20) | copy-start | bytes 20740
  13.4 18.7 %copy-start = (s32[2]{0:T(128)S(1)}, s32[2]{0:T(128)}, u32[]{:S(2)}) copy-start(s32[2]{0:T(128)} %length_ref.1) | copy-start | bytes 28
  13.4 8.0 %collective-permute-start.3 = (bf16[24,7296]{1,0:T(8,128)(2,1)S(1)}, bf16[24,7296]{1,0:T(8,128)(2,1)S(1)}, u32[]{:S(2)}, u32[]{:S(2)}) collective-permute-start(bf16[24,7296]{1,0:T(8,128)(2,1)S(1)} %stack.8.refs_0_), channel_id=1, source_target_pairs={{0,48},{1,49},{2,50},{3,51},{4,52},{5,53},{6,54},{7,55},{8,56},{9,... | collective-permute-start | bytes 1050632 | tf_op jit(solution)/shard_map/ppermute | solution.py:44
  16.5 12.3 %collective-permute-start.4 = (bf16[24,7296]{1,0:T(8,128)(2,1)S(1)}, bf16[24,7296]{1,0:T(8,128)(2,1)S(1)}, u32[]{:S(2)}, u32[]{:S(2)}) collective-permute-start(bf16[24,7296]{1,0:T(8,128)(2,1)S(1)} %stack.8.refs_0_), channel_id=1, source_target_pairs={{0,16},{1,17},{2,18},{3,19},{4,20},{5,21},{6,22},{7,23},{8,24},{9,... | collective-permute-start | bytes 1050632 | tf_op jit(solution)/shard_map/ppermute | solution.py:44
  16.5 12.3 %collective-permute-start.5 = (bf16[24,7296]{1,0:T(8,128)(2,1)S(1)}, bf16[24,7296]{1,0:T(8,128)(2,1)S(1)}, u32[]{:S(2)}, u32[]{:S(2)}) collective-permute-start(bf16[24,7296]{1,0:T(8,128)(2,1)S(1)} %stack.8.refs_0_), channel_id=1, source_target_pairs={{0,32},{1,33},{2,34},{3,35},{4,36},{5,37},{6,38},{7,39},{8,40},{9,... | collective-permute-start | bytes 1050632 | tf_op jit(solution)/shard_map/ppermute | solution.py:44
  21.4 19.1 %collective-permute-start.6 = (bf16[48,7296]{1,0:T(8,128)(2,1)S(1)}, bf16[48,7296]{1,0:T(8,128)(2,1)S(1)}, u32[]{:S(2)}, u32[]{:S(2)}) collective-permute-start(bf16[48,7296]{1,0:T(8,128)(2,1)S(1)} %stack.9.refs_0_), channel_id=1, source_target_pairs={{0,3},{1,0},{2,1},{3,2},{4,7},{5,4},{6,5},{7,6},{8,11},{9,8},{10,9... | collective-permute-start | bytes 2101256 | tf_op jit(solution)/shard_map/ppermute | solution.py:44
  24.2 16.2 %collective-permute-start.7 = (bf16[48,7296]{1,0:T(8,128)(2,1)S(1)}, bf16[48,7296]{1,0:T(8,128)(2,1)S(1)}, u32[]{:S(2)}, u32[]{:S(2)}) collective-permute-start(bf16[48,7296]{1,0:T(8,128)(2,1)S(1)} %stack.9.refs_0_), channel_id=1, source_target_pairs={{0,1},{1,2},{2,3},{3,0},{4,5},{5,6},{6,7},{7,4},{8,9},{9,10},{10,1... | collective-permute-start | bytes 2101256 | tf_op jit(solution)/shard_map/ppermute | solution.py:44
  28.8 15.9 %collective-permute-start.8 = (bf16[48,7296]{1,0:T(8,128)(2,1)S(1)}, bf16[48,7296]{1,0:T(8,128)(2,1)S(1)}, u32[]{:S(2)}, u32[]{:S(2)}) collective-permute-start(bf16[48,7296]{1,0:T(8,128)(2,1)S(1)} %stack.10.refs_1_), channel_id=1, source_target_pairs={{0,3},{1,0},{2,1},{3,2},{4,7},{5,4},{6,5},{7,6},{8,11},{9,8},{10,9... | collective-permute-start | bytes 2101256 | tf_op jit(solution)/shard_map/ppermute | solution.py:44
  32.1 12.7 %collective-permute-start.9 = (bf16[48,7296]{1,0:T(8,128)(2,1)S(1)}, bf16[48,7296]{1,0:T(8,128)(2,1)S(1)}, u32[]{:S(2)}, u32[]{:S(2)}) collective-permute-start(bf16[48,7296]{1,0:T(8,128)(2,1)S(1)} %stack.10.refs_1_), channel_id=1, source_target_pairs={{0,1},{1,2},{2,3},{3,0},{4,5},{5,6},{6,7},{7,4},{8,9},{9,10},{10,1... | collective-permute-start | bytes 2101256 | tf_op jit(solution)/shard_map/ppermute | solution.py:44
  44.9 3.2 %collective-permute-start.12 = (bf16[96,7296]{1,0:T(8,128)(2,1)S(1)}, bf16[96,7296]{1,0:T(8,128)(2,1)S(1)}, u32[]{:S(2)}, u32[]{:S(2)}) collective-permute-start(bf16[96,7296]{1,0:T(8,128)(2,1)S(1)} %stack.13), channel_id=1, source_target_pairs={{0,64},{64,0},{1,65},{65,1},{2,66},{66,2},{3,67},{67,3},{4,68},{68... | collective-permute-start | bytes 4202504 | tf_op jit(solution)/shard_map/ppermute | solution.py:48
  45.1 8.9 %collective-permute-start.11 = (bf16[96,7296]{1,0:T(8,128)(2,1)S(1)}, bf16[96,7296]{1,0:T(8,128)(2,1)S(1)}, u32[]{:S(2)}, u32[]{:S(2)}) collective-permute-start(bf16[96,7296]{1,0:T(8,128)(2,1)S(1)} %stack.12), channel_id=1, source_target_pairs={{0,64},{64,0},{1,65},{65,1},{2,66},{66,2},{3,67},{67,3},{4,68},{68... | collective-permute-start | bytes 4202504 | tf_op jit(solution)/shard_map/ppermute | solution.py:48
  45.6 13.1 %collective-permute-start.10 = (bf16[96,7296]{1,0:T(8,128)(2,1)S(1)}, bf16[96,7296]{1,0:T(8,128)(2,1)S(1)}, u32[]{:S(2)}, u32[]{:S(2)}) collective-permute-start(bf16[96,7296]{1,0:T(8,128)(2,1)S(1)} %get-tuple-element.33.refs_0_), channel_id=1, source_target_pairs={{0,64},{64,0},{1,65},{65,1},{2,66},{66,2},{3,67},{67,3},{4,68},{68... | collective-permute-start | bytes 4202504 | tf_op jit(solution)/shard_map/ppermute | solution.py:48
  50.6 10.8 %collective-permute-start.14 = (bf16[96,7168]{1,0:T(8,128)(2,1)S(1)}, bf16[96,7168]{1,0:T(8,128)(2,1)S(1)}, u32[]{:S(2)}, u32[]{:S(2)}) collective-permute-start(bf16[96,7168]{1,0:T(8,128)(2,1)S(1)} %get-tuple-element.42), channel_id=1, source_target_pairs={{0,64},{64,0},{1,65},{65,1},{2,66},{66,2},{3,67},{67,3},{4,68},{68... | collective-permute-start | bytes 4128776 | tf_op jit(solution)/shard_map/ppermute | solution.py:48
  50.8 14.8 %collective-permute-start.21 = (bf16[48,7296]{1,0:T(8,128)(2,1)S(1)}, bf16[48,7296]{1,0:T(8,128)(2,1)S(1)}, u32[]{:S(2)}, u32[]{:S(2)}) collective-permute-start(bf16[48,7296]{1,0:T(8,128)(2,1)S(1)} %get-tuple-element.36.refs_0_), channel_id=1, source_target_pairs={{0,3},{1,0},{2,1},{3,2},{4,7},{5,4},{6,5},{7,6},{8,11},{9,8},{10,9... | collective-permute-start | bytes 2101256 | tf_op jit(solution)/shard_map/ppermute | solution.py:44
  54.0 12.3 %collective-permute-start.22 = (bf16[48,7296]{1,0:T(8,128)(2,1)S(1)}, bf16[48,7296]{1,0:T(8,128)(2,1)S(1)}, u32[]{:S(2)}, u32[]{:S(2)}) collective-permute-start(bf16[48,7296]{1,0:T(8,128)(2,1)S(1)} %get-tuple-element.35.refs_1_), channel_id=1, source_target_pairs={{0,1},{1,2},{2,3},{3,0},{4,5},{5,6},{6,7},{7,4},{8,9},{9,10},{10,1... | collective-permute-start | bytes 2101256 | tf_op jit(solution)/shard_map/ppermute | solution.py:44
  56.5 5.2 %collective-permute-start.15 = (bf16[96,7168]{1,0:T(8,128)(2,1)S(1)}, bf16[96,7168]{1,0:T(8,128)(2,1)S(1)}, u32[]{:S(2)}, u32[]{:S(2)}) collective-permute-start(bf16[96,7168]{1,0:T(8,128)(2,1)S(1)} %get-tuple-element.43), channel_id=1, source_target_pairs={{0,64},{64,0},{1,65},{65,1},{2,66},{66,2},{3,67},{67,3},{4,68},{68... | collective-permute-start | bytes 4128776 | tf_op jit(solution)/shard_map/ppermute | solution.py:48
  61.2 11.7 %collective-permute-start.13 = (bf16[96,7168]{1,0:T(8,128)(2,1)S(1)}, bf16[96,7168]{1,0:T(8,128)(2,1)S(1)}, u32[]{:S(2)}, u32[]{:S(2)}) collective-permute-start(bf16[96,7168]{1,0:T(8,128)(2,1)S(1)} %get-tuple-element.41), channel_id=1, source_target_pairs={{0,64},{64,0},{1,65},{65,1},{2,66},{66,2},{3,67},{67,3},{4,68},{68... | collective-permute-start | bytes 4128776 | tf_op jit(solution)/shard_map/ppermute | solution.py:48
  62.1 19.6 %collective-permute-start.16 = (bf16[96,7168]{1,0:T(8,128)(2,1)S(1)}, bf16[96,7168]{1,0:T(8,128)(2,1)S(1)}, u32[]{:S(2)}, u32[]{:S(2)}) collective-permute-start(bf16[96,7168]{1,0:T(8,128)(2,1)S(1)} %stack.14), channel_id=1, source_target_pairs={{0,1},{1,2},{2,3},{3,0},{4,5},{5,6},{6,7},{7,4},{8,9},{9,10},{10,1... | collective-permute-start | bytes 4128776 | tf_op jit(solution)/shard_map/ppermute | solution.py:44
  62.3 19.4 %collective-permute-start.17 = (bf16[96,7168]{1,0:T(8,128)(2,1)S(1)}, bf16[96,7168]{1,0:T(8,128)(2,1)S(1)}, u32[]{:S(2)}, u32[]{:S(2)}) collective-permute-start(bf16[96,7168]{1,0:T(8,128)(2,1)S(1)} %stack.15), channel_id=1, source_target_pairs={{0,3},{1,0},{2,1},{3,2},{4,7},{5,4},{6,5},{7,6},{8,11},{9,8},{10,9... | collective-permute-start | bytes 4128776 | tf_op jit(solution)/shard_map/ppermute | solution.py:44
  66.3 3.1 %collective-permute-start.23 = (bf16[48,7296]{1,0:T(8,128)(2,1)S(1)}, bf16[48,7296]{1,0:T(8,128)(2,1)S(1)}, u32[]{:S(2)}, u32[]{:S(2)}) collective-permute-start(bf16[48,7296]{1,0:T(8,128)(2,1)S(1)} %get-tuple-element.46.refs_0_), channel_id=1, source_target_pairs={{0,64},{64,0},{1,65},{65,1},{2,66},{66,2},{3,67},{67,3},{4,68},{68... | collective-permute-start | bytes 2101256 | tf_op jit(solution)/shard_map/ppermute | solution.py:48
  67.6 2.8 %collective-permute-start.24 = (bf16[48,7296]{1,0:T(8,128)(2,1)S(1)}, bf16[48,7296]{1,0:T(8,128)(2,1)S(1)}, u32[]{:S(2)}, u32[]{:S(2)}) collective-permute-start(bf16[48,7296]{1,0:T(8,128)(2,1)S(1)} %get-tuple-element.47.refs_1_), channel_id=1, source_target_pairs={{0,64},{64,0},{1,65},{65,1},{2,66},{66,2},{3,67},{67,3},{4,68},{68... | collective-permute-start | bytes 2101256 | tf_op jit(solution)/shard_map/ppermute | solution.py:48
  81.7 2.1 %collective-permute-start.25 = (bf16[48,7168]{1,0:T(8,128)(2,1)S(1)}, bf16[48,7168]{1,0:T(8,128)(2,1)S(1)}, u32[]{:S(2)}, u32[]{:S(2)}) collective-permute-start(bf16[48,7168]{1,0:T(8,128)(2,1)S(1)} %get-tuple-element.52), channel_id=1, source_target_pairs={{0,64},{64,0},{1,65},{65,1},{2,66},{66,2},{3,67},{67,3},{4,68},{68... | collective-permute-start | bytes 2064392 | tf_op jit(solution)/shard_map/ppermute | solution.py:48
  82.0 2.8 %collective-permute-start.26 = (bf16[48,7168]{1,0:T(8,128)(2,1)S(1)}, bf16[48,7168]{1,0:T(8,128)(2,1)S(1)}, u32[]{:S(2)}, u32[]{:S(2)}) collective-permute-start(bf16[48,7168]{1,0:T(8,128)(2,1)S(1)} %get-tuple-element.53), channel_id=1, source_target_pairs={{0,64},{64,0},{1,65},{65,1},{2,66},{66,2},{3,67},{67,3},{4,68},{68... | collective-permute-start | bytes 2064392 | tf_op jit(solution)/shard_map/ppermute | solution.py:48
  85.1 9.0 %collective-permute-start.29 = (bf16[24,7168]{1,0:T(8,128)(2,1)S(1)}, bf16[24,7168]{1,0:T(8,128)(2,1)S(1)}, u32[]{:S(2)}, u32[]{:S(2)}) collective-permute-start(bf16[24,7168]{1,0:T(8,128)(2,1)S(1)} %get-tuple-element.57), channel_id=1, source_target_pairs={{0,32},{1,33},{2,34},{3,35},{4,36},{5,37},{6,38},{7,39},{8,40},{9,... | collective-permute-start | bytes 1032200 | tf_op jit(solution)/shard_map/ppermute | solution.py:44
  87.3 10.7 %collective-permute-start.28 = (bf16[24,7168]{1,0:T(8,128)(2,1)S(1)}, bf16[24,7168]{1,0:T(8,128)(2,1)S(1)}, u32[]{:S(2)}, u32[]{:S(2)}) collective-permute-start(bf16[24,7168]{1,0:T(8,128)(2,1)S(1)} %get-tuple-element.56), channel_id=1, source_target_pairs={{0,48},{1,49},{2,50},{3,51},{4,52},{5,53},{6,54},{7,55},{8,56},{9,... | collective-permute-start | bytes 1032200 | tf_op jit(solution)/shard_map/ppermute | solution.py:44
  88.2 9.7 %collective-permute-start.27 = (bf16[24,7168]{1,0:T(8,128)(2,1)S(1)}, bf16[24,7168]{1,0:T(8,128)(2,1)S(1)}, u32[]{:S(2)}, u32[]{:S(2)}) collective-permute-start(bf16[24,7168]{1,0:T(8,128)(2,1)S(1)} %get-tuple-element.55), channel_id=1, source_target_pairs={{0,16},{1,17},{2,18},{3,19},{4,20},{5,21},{6,22},{7,23},{8,24},{9,... | collective-permute-start | bytes 1032200 | tf_op jit(solution)/shard_map/ppermute | solution.py:44
  89.7 11.8 %collective-permute-start.20 = (bf16[24,7168]{1,0:T(8,128)(2,1)S(1)}, bf16[24,7168]{1,0:T(8,128)(2,1)S(1)}, u32[]{:S(2)}, u32[]{:S(2)}) collective-permute-start(bf16[24,7168]{1,0:T(8,128)(2,1)S(1)} %get-tuple-element.59), channel_id=1, source_target_pairs={{0,32},{1,33},{2,34},{3,35},{4,36},{5,37},{6,38},{7,39},{8,40},{9,... | collective-permute-start | bytes 1032200 | tf_op jit(solution)/shard_map/ppermute | solution.py:44
  91.5 16.5 %collective-permute-start.19 = (bf16[24,7168]{1,0:T(8,128)(2,1)S(1)}, bf16[24,7168]{1,0:T(8,128)(2,1)S(1)}, u32[]{:S(2)}, u32[]{:S(2)}) collective-permute-start(bf16[24,7168]{1,0:T(8,128)(2,1)S(1)} %get-tuple-element.60), channel_id=1, source_target_pairs={{0,48},{1,49},{2,50},{3,51},{4,52},{5,53},{6,54},{7,55},{8,56},{9,... | collective-permute-start | bytes 1032200 | tf_op jit(solution)/shard_map/ppermute | solution.py:44
  94.2 13.9 %collective-permute-start.18 = (bf16[24,7168]{1,0:T(8,128)(2,1)S(1)}, bf16[24,7168]{1,0:T(8,128)(2,1)S(1)}, u32[]{:S(2)}, u32[]{:S(2)}) collective-permute-start(bf16[24,7168]{1,0:T(8,128)(2,1)S(1)} %get-tuple-element.58), channel_id=1, source_target_pairs={{0,16},{1,17},{2,18},{3,19},{4,20},{5,21},{6,22},{7,23},{8,24},{9,... | collective-permute-start | bytes 1032200 | tf_op jit(solution)/shard_map/ppermute | solution.py:44
  98.2 9.9 %collective-permute-start.30 = (bf16[24,7168]{1,0:T(8,128)(2,1)S(1)}, bf16[24,7168]{1,0:T(8,128)(2,1)S(1)}, u32[]{:S(2)}, u32[]{:S(2)}) collective-permute-start(bf16[24,7168]{1,0:T(8,128)(2,1)S(1)} %add_convert_fusion.6), channel_id=1, source_target_pairs={{0,2},{1,3},{2,0},{3,1},{4,6},{5,7},{6,4},{7,5},{8,10},{9,11},{10,... | collective-permute-start | bytes 1032200 | tf_op jit(solution)/shard_map/ppermute | solution.py:44
  108.5 6.4 %collective-permute-start.33 = (bf16[6,7168]{1,0:T(8,128)(2,1)S(1)}, bf16[6,7168]{1,0:T(8,128)(2,1)S(1)}, u32[]{:S(2)}, u32[]{:S(2)}) collective-permute-start(bf16[6,7168]{1,0:T(8,128)(2,1)S(1)} %get-tuple-element.66), channel_id=1, source_target_pairs={{0,8},{1,9},{2,10},{3,11},{4,12},{5,13},{6,14},{7,15},{8,0},{9,1},... | collective-permute-start | bytes 258056 | tf_op jit(solution)/shard_map/ppermute | solution.py:44
  108.9 9.3 %collective-permute-start.32 = (bf16[6,7168]{1,0:T(8,128)(2,1)S(1)}, bf16[6,7168]{1,0:T(8,128)(2,1)S(1)}, u32[]{:S(2)}, u32[]{:S(2)}) collective-permute-start(bf16[6,7168]{1,0:T(8,128)(2,1)S(1)} %get-tuple-element.67), channel_id=1, source_target_pairs={{0,12},{1,13},{2,14},{3,15},{4,0},{5,1},{6,2},{7,3},{8,4},{9,5},{1... | collective-permute-start | bytes 258056 | tf_op jit(solution)/shard_map/ppermute | solution.py:44
  113.3 6.0 %collective-permute-start.31 = (bf16[6,7168]{1,0:T(8,128)(2,1)S(1)}, bf16[6,7168]{1,0:T(8,128)(2,1)S(1)}, u32[]{:S(2)}, u32[]{:S(2)}) collective-permute-start(bf16[6,7168]{1,0:T(8,128)(2,1)S(1)} %get-tuple-element.65), channel_id=1, source_target_pairs={{0,4},{1,5},{2,6},{3,7},{4,8},{5,9},{6,10},{7,11},{8,12},{9,13},{1... | collective-permute-start | bytes 258056 | tf_op jit(solution)/shard_map/ppermute | solution.py:44
where the time goes:
time: 121 us; the launch traced here: 120 us
  waiting for transfers between devices  46.7 us (39%)
  starting transfers between devices  45.3 us (37%)
  Pallas kernels  24.5 us (20%)
  other arithmetic  1.91 us (2%)
    ppermute x24, starting transfers between devices, shift(): return lax.ppermute(block, AXES, shifted_pairs(axis_of_core, distance))  40.2 us
    ppermute x24, waiting for transfers between devices, shift(): return lax.ppermute(block, AXES, shifted_pairs(axis_of_core, distance))  39.2 us
    pallas_call x4, Pallas kernels, expert_call(): pl.pallas_call(functools.partial(expert_body, count=count), out_shape=[ja...  9.87 us
    pallas_call x1, Pallas kernels, attend(): pl.pallas_call(attend_body, out_shape=jax.ShapeDtypeStruct((steps, reques...  8.25 us
    ppermute x10, waiting for transfers between devices, other_core(): return lax.ppermute(block, 'c', [(0, 1), (1, 0)])  7.46 us
    ppermute x10, starting transfers between devices, other_core(): return lax.ppermute(block, 'c', [(0, 1), (1, 0)])  5.13 us
    pallas_call x1, Pallas kernels, resident(): pl.pallas_call(functools.partial(resident_body, count=count), out_shape=[...  4.23 us
  transfers between devices with their start and end apart: 34, of which 17 were waited for; matrix products, arithmetic and copies ran while one was open for 1% of the time, Pallas kernels for 19%

commit v1 on v0

--- a/solution.py
+++ b/solution.py
@@ -353,12 +353,13 @@
     weights = resident([w_gate, w_up, w_down], [in_hbm(attended), *arrived[:2]])
     own, *arrived = hold([stack([first, second]), *arrived], weights)
     opposite = [shift(arrived[0], far, -1), shift(arrived[3], far, 1)]
-    outs, back = apply_expert(arrived[:2], [])
-    sums = merge(outs, back)
-    outs, back = apply_expert(arrived[2:], outs[:1])
-    sums += merge(outs, back)
+    theirs = [other_core(stack(pair)) for pair in (arrived[:2], arrived[2:])]
+    outs = expert_call(arrived, weights, [])
+    back_first = expert_call(theirs[:1], weights, outs[:1])
+    back_second = expert_call(theirs[1:], weights, back_first)
+    sums = merge(outs[:2], other_core(back_first[0])) + merge(outs[2:], other_core(back_second[0]))
     home = [shift(stack(sums[0::2]), far, 1), shift(stack(sums[1::2]), far, -1)]
-    own_out, own_back = apply_expert([own], outs[:1])
+    own_out, own_back = apply_expert([own], back_second)
     opposite = hold(opposite, [*sums, *own_out])
     theirs = [other_core(block) for block in opposite]
     outs = expert_call([*opposite, *theirs], weights, own_out)

time: 121 us -> 120 us (level)
  Pallas kernels: 24.5 us -> 26 us
  waiting for transfers between devices: 46.7 us -> 45.3 us
    ppermute x10, waiting for transfers between devices: 7.46 us -> 5.12 us  [other_core(): return lax.ppermute(block, 'c', [(0, 1), (1, 0)])]
    pallas_call x4 -> x5, Pallas kernels: 9.87 us -> 11.4 us  [expert_call(): pl.pallas_call(functools.partial(expert_body, count=count), out_shape=[ja...]
  transfers between devices with their start and end apart: 34 -> 34, of which waited for: 17 -> 18; matrix products, arithmetic and copies ran while one was open for 1% -> 1% of each run, Pallas kernels for 19% -> 20%
where the time goes in v1:
time: 120 us
  waiting for transfers between devices  45.3 us (38%)
  starting transfers between devices  45 us (38%)
  Pallas kernels  26 us (22%)
  other arithmetic  1.96 us (2%)
    ppermute x24, waiting for transfers between devices, shift(): return lax.ppermute(block, AXES, shifted_pairs(axis_of_core, distance))  40.2 us
    ppermute x24, starting transfers between devices, shift(): return lax.ppermute(block, AXES, shifted_pairs(axis_of_core, distance))  39.8 us
    pallas_call x5, Pallas kernels, expert_call(): pl.pallas_call(functools.partial(expert_body, count=count), out_shape=[ja...  11.4 us
    pallas_call x1, Pallas kernels, attend(): pl.pallas_call(attend_body, out_shape=jax.ShapeDtypeStruct((steps, reques...  8.25 us
    ppermute x10, starting transfers between devices, other_core(): return lax.ppermute(block, 'c', [(0, 1), (1, 0)])  5.14 us
    ppermute x10, waiting for transfers between devices, other_core(): return lax.ppermute(block, 'c', [(0, 1), (1, 0)])  5.12 us
    pallas_call x1, Pallas kernels, resident(): pl.pallas_call(functools.partial(resident_body, count=count), out_shape=[...  4.23 us
  transfers between devices with their start and end apart: 34, of which 18 were waited for; matrix products, arithmetic and copies ran while one was open for 1% of the time, Pallas kernels for 20%

profile of v1, /device:TPU:0, one launch (start us, length us, event | category | flops | bytes accessed | tf_op | source)
XLA Modules:
  0.0 120.0 jit_solution(1327082995688630272)
XLA Ops:
  0.6 1.2 prepare.1.refs_0_
  1.8 4.2 %collective-permute-start = (bf16[6,7296]{1,0:T(8,128)(2,1)S(1)}, bf16[6,7296]{1,0:T(8,128)(2,1)S(1)}, u32[]{:S(2)}, u32[]{:S(2)}) collective-permute-start(bf16[6,7296]{1,0:T(8,128)(2,1)S(1)} %prepare.1.refs_0_), channel_id=1, source_target_pairs={{0,12},{1,13},{2,14},{3,15},{4,0},{5,1},{6,2},{7,3},{8,4},{9,5},{1... | collective-permute-start | bytes 262664 | tf_op jit(solution)/shard_map/ppermute | solution.py:44
  6.0 1.9 %collective-permute-start.2 = (bf16[6,7296]{1,0:T(8,128)(2,1)S(1)}, bf16[6,7296]{1,0:T(8,128)(2,1)S(1)}, u32[]{:S(2)}, u32[]{:S(2)}) collective-permute-start(bf16[6,7296]{1,0:T(8,128)(2,1)S(1)} %prepare.1.refs_0_), channel_id=1, source_target_pairs={{0,8},{1,9},{2,10},{3,11},{4,12},{5,13},{6,14},{7,15},{8,0},{9,1},... | collective-permute-start | bytes 262664 | tf_op jit(solution)/shard_map/ppermute | solution.py:44
  7.9 0.5 collective-permute-done.refs_1_
  8.4 4.9 %collective-permute-done.1.refs_2_ = bf16[6,7296]{1,0:T(8,128)(2,1)S(1)} collective-permute-done((bf16[6,7296]{1,0:T(8,128)(2,1)S(1)}, bf16[6,7296]{1,0:T(8,128)(2,1)S(1)}, u32[]{:S(2)}, u32[]{:S(2)}) %collective-permute-start.1) | collective-permute-done | bytes 87584 | tf_op jit(solution)/shard_map/ppermute | solution.py:44
  13.4 3.1 %collective-permute-start.3 = (bf16[24,7296]{1,0:T(8,128)(2,1)S(1)}, bf16[24,7296]{1,0:T(8,128)(2,1)S(1)}, u32[]{:S(2)}, u32[]{:S(2)}) collective-permute-start(bf16[24,7296]{1,0:T(8,128)(2,1)S(1)} %stack.8.refs_0_), channel_id=1, source_target_pairs={{0,48},{1,49},{2,50},{3,51},{4,52},{5,53},{6,54},{7,55},{8,56},{9,... | collective-permute-start | bytes 1050632 | tf_op jit(solution)/shard_map/ppermute | solution.py:44
  16.5 2.2 %collective-permute-start.5 = (bf16[24,7296]{1,0:T(8,128)(2,1)S(1)}, bf16[24,7296]{1,0:T(8,128)(2,1)S(1)}, u32[]{:S(2)}, u32[]{:S(2)}) collective-permute-start(bf16[24,7296]{1,0:T(8,128)(2,1)S(1)} %stack.8.refs_0_), channel_id=1, source_target_pairs={{0,32},{1,33},{2,34},{3,35},{4,36},{5,37},{6,38},{7,39},{8,40},{9,... | collective-permute-start | bytes 1050632 | tf_op jit(solution)/shard_map/ppermute | solution.py:44
  18.7 2.7 %collective-permute-done.3.refs_1_ = bf16[24,7296]{1,0:T(8,128)(2,1)S(1)} collective-permute-done((bf16[24,7296]{1,0:T(8,128)(2,1)S(1)}, bf16[24,7296]{1,0:T(8,128)(2,1)S(1)}, u32[]{:S(2)}, u32[]{:S(2)}) %collective-permute-start.3) | collective-permute-done | bytes 350240 | tf_op jit(solution)/shard_map/ppermute | solution.py:44
  21.4 2.8 %collective-permute-start.6 = (bf16[48,7296]{1,0:T(8,128)(2,1)S(1)}, bf16[48,7296]{1,0:T(8,128)(2,1)S(1)}, u32[]{:S(2)}, u32[]{:S(2)}) collective-permute-start(bf16[48,7296]{1,0:T(8,128)(2,1)S(1)} %stack.9.refs_0_), channel_id=1, source_target_pairs={{0,3},{1,0},{2,1},{3,2},{4,7},{5,4},{6,5},{7,6},{8,11},{9,8},{10,9... | collective-permute-start | bytes 2101256 | tf_op jit(solution)/shard_map/ppermute | solution.py:44
  24.2 4.5 %collective-permute-done.4.refs_0_ = bf16[24,7296]{1,0:T(8,128)(2,1)S(1)} collective-permute-done((bf16[24,7296]{1,0:T(8,128)(2,1)S(1)}, bf16[24,7296]{1,0:T(8,128)(2,1)S(1)}, u32[]{:S(2)}, u32[]{:S(2)}) %collective-permute-start.4) | collective-permute-done | bytes 350240 | tf_op jit(solution)/shard_map/ppermute | solution.py:44
  28.8 3.3 %collective-permute-start.8 = (bf16[48,7296]{1,0:T(8,128)(2,1)S(1)}, bf16[48,7296]{1,0:T(8,128)(2,1)S(1)}, u32[]{:S(2)}, u32[]{:S(2)}) collective-permute-start(bf16[48,7296]{1,0:T(8,128)(2,1)S(1)} %stack.10.refs_1_), channel_id=1, source_target_pairs={{0,3},{1,0},{2,1},{3,2},{4,7},{5,4},{6,5},{7,6},{8,11},{9,8},{10,9... | collective-permute-start | bytes 2101256 | tf_op jit(solution)/shard_map/ppermute | solution.py:44
  32.1 8.3 %attend.1.refs_3_ = bf16[3,2,128,512]{3,2,1,0:T(8,128)(2,1)} custom-call(s32[2]{0:T(128)S(1)} %copy-done, bf16[3,2,576,128]{3,2,1,0:T(8,128)(2,1)} %bitcast.9, bf16[2,576,2048]{2,1,0:T(8,128)(2,1)} %bitcast.8, bf16[2,16,576]{2,1,0:T(8,128)(2,1)S(1)} %pad.4.fresh_ref), custom_call_target="tpu_custom_call" | custom-call | flops 3422552064 | bytes 6389760 | tf_op jit(solution)/shard_map/attend/pallas_call | solution.py:191
  40.4 0.1 stack.11.refs_0_
  40.5 4.2 %resident.1 = (bf16[7168,256]{1,0:T(8,128)(2,1)S(1)}, bf16[7168,256]{1,0:T(8,128)(2,1)S(1)}, bf16[256,7168]{1,0:T(8,128)(2,1)S(1)}) custom-call(bf16[7168,256]{1,0:T(8,128)(2,1)} %refs_0_.1, bf16[7168,256]{1,0:T(8,128)(2,1)} %refs_1_.1, bf16[256,7168]{1,0:T(8,128)(2,1)} %refs_2_.1, bf16[3,2,128,512]{3,2,1,0:T(8,128)(2,1)} %attend.1.refs_3_, ...), custom_call_target="tpu_custom_call" | custom-call | tf_op jit(solution)/shard_map/resident/pallas_call | solution.py:264
  44.8 0.1 stack.13
  44.9 0.1 collective-permute-start.12
  45.0 0.1 stack.12
  45.1 0.6 collective-permute-start.11
  45.6 0.1 collective-permute-start.10
  45.7 2.4 %experts.5 = (bf16[48,7168]{1,0:T(8,128)(2,1)S(1)}, bf16[48,7168]{1,0:T(8,128)(2,1)S(1)}, bf16[48,7168]{1,0:T(8,128)(2,1)S(1)}, bf16[48,7168]{1,0:T(8,128)(2,1)S(1)}) custom-call(bf16[48,7296]{1,0:T(8,128)(2,1)S(1)} %get-tuple-element.34.refs_0_, bf16[48,7296]{1,0:T(8,128)(2,1)S(1)} %get-tuple-element.35.refs_1_, ...), custom_call_target="tpu_custom_call" | custom-call | flops 2113929216 | bytes 5505024 | tf_op jit(solution)/shard_map/experts/pallas_call | solution.py:316
  48.2 2.0 %experts.6.refs_4_ = bf16[96,7168]{1,0:T(8,128)(2,1)S(1)} custom-call(bf16[96,7296]{1,0:T(8,128)(2,1)S(1)} %collective-permute-done.12.refs_0_, bf16[7168,256]{1,0:T(8,128)(2,1)S(1)} %get-tuple-element.28.refs_5_.refs_4_.refs_1_.refs_2_, bf16[7168,256]{1,0:T(8,128)(2,1)S(1)} %get-tuple-element.29.refs_6_.refs_5_.refs_2_.refs_3_, ...), custom_call_target="tpu_custom_call" | custom-call | flops 1056964608 | bytes 2752512 | tf_op jit(solution)/shard_map/experts/pallas_call | solution.py:316
  50.2 0.5 collective-permute-start.14
  50.7 3.2 %collective-permute-start.21 = (bf16[48,7296]{1,0:T(8,128)(2,1)S(1)}, bf16[48,7296]{1,0:T(8,128)(2,1)S(1)}, u32[]{:S(2)}, u32[]{:S(2)}) collective-permute-start(bf16[48,7296]{1,0:T(8,128)(2,1)S(1)} %get-tuple-element.34.refs_0_), channel_id=1, source_target_pairs={{0,3},{1,0},{2,1},{3,2},{4,7},{5,4},{6,5},{7,6},{8,11},{9,8},{10,9... | collective-permute-start | bytes 2101256 | tf_op jit(solution)/shard_map/ppermute | solution.py:44
  53.9 2.0 %experts.7.refs_5_ = bf16[96,7168]{1,0:T(8,128)(2,1)S(1)} custom-call(bf16[96,7296]{1,0:T(8,128)(2,1)S(1)} %collective-permute-done.11.refs_0_, bf16[7168,256]{1,0:T(8,128)(2,1)S(1)} %get-tuple-element.28.refs_5_.refs_4_.refs_1_.refs_2_, bf16[7168,256]{1,0:T(8,128)(2,1)S(1)} %get-tuple-element.29.refs_6_.refs_5_.refs_2_.refs_3_, ...), custom_call_target="tpu_custom_call" | custom-call | flops 1056964608 | bytes 2752512 | tf_op jit(solution)/shard_map/experts/pallas_call | solution.py:316
  55.9 2.0 %collective-permute-start.15 = (bf16[96,7168]{1,0:T(8,128)(2,1)S(1)}, bf16[96,7168]{1,0:T(8,128)(2,1)S(1)}, u32[]{:S(2)}, u32[]{:S(2)}) collective-permute-start(bf16[96,7168]{1,0:T(8,128)(2,1)S(1)} %experts.7.refs_5_), channel_id=1, source_target_pairs={{0,64},{64,0},{1,65},{65,1},{2,66},{66,2},{3,67},{67,3},{4,68},{68... | collective-permute-start | bytes 4128776 | tf_op jit(solution)/shard_map/ppermute | solution.py:48
  57.9 2.5 %experts.8 = (bf16[96,7168]{1,0:T(8,128)(2,1)S(1)}, bf16[96,7168]{1,0:T(8,128)(2,1)S(1)}) custom-call(bf16[96,7296]{1,0:T(8,128)(2,1)S(1)} %get-tuple-element.31.refs_0_, bf16[96,7296]{1,0:T(8,128)(2,1)S(1)} %collective-permute-done.10.refs_1_, bf16[7168,256]{1,0:T(8,128)(2,1)S(1)} %get-tuple-element.28.refs_5_.refs_4_.refs_1_.refs_2_, ...), custom_call_target="tpu_custom_call" | custom-call | flops 2113929216 | bytes 5505024 | tf_op jit(solution)/shard_map/experts/pallas_call | solution.py:316
  60.4 0.1 collective-permute-start.13
  60.5 0.4 add_convert_fusion.2
  60.8 0.3 add_convert_fusion.1
  61.2 0.1 stack.14
  61.4 0.1 stack.15
  61.5 3.3 %collective-permute-start.17 = (bf16[96,7168]{1,0:T(8,128)(2,1)S(1)}, bf16[96,7168]{1,0:T(8,128)(2,1)S(1)}, u32[]{:S(2)}, u32[]{:S(2)}) collective-permute-start(bf16[96,7168]{1,0:T(8,128)(2,1)S(1)} %stack.15), channel_id=1, source_target_pairs={{0,3},{1,0},{2,1},{3,2},{4,7},{5,4},{6,5},{7,6},{8,11},{9,8},{10,9... | collective-permute-start | bytes 4128776 | tf_op jit(solution)/shard_map/ppermute | solution.py:44
  64.8 1.4 %collective-permute-done.22.refs_1_ = bf16[48,7296]{1,0:T(8,128)(2,1)S(1)} collective-permute-done((bf16[48,7296]{1,0:T(8,128)(2,1)S(1)}, bf16[48,7296]{1,0:T(8,128)(2,1)S(1)}, u32[]{:S(2)}, u32[]{:S(2)}) %collective-permute-start.22) | collective-permute-done | bytes 700448 | tf_op jit(solution)/shard_map/ppermute | solution.py:44
  66.2 1.0 collective-permute-start.23
  67.2 1.8 %collective-permute-done.23.refs_2_ = bf16[48,7296]{1,0:T(8,128)(2,1)S(1)} collective-permute-done((bf16[48,7296]{1,0:T(8,128)(2,1)S(1)}, bf16[48,7296]{1,0:T(8,128)(2,1)S(1)}, u32[]{:S(2)}, u32[]{:S(2)}) %collective-permute-start.23) | collective-permute-done | bytes 700448 | tf_op jit(solution)/shard_map/ppermute | solution.py:48
  69.0 1.0 collective-permute-done.24.refs_3_
  70.0 2.5 %experts.9 = (bf16[48,7168]{1,0:T(8,128)(2,1)S(1)}, bf16[48,7168]{1,0:T(8,128)(2,1)S(1)}, bf16[48,7168]{1,0:T(8,128)(2,1)S(1)}, bf16[48,7168]{1,0:T(8,128)(2,1)S(1)}) custom-call(bf16[48,7296]{1,0:T(8,128)(2,1)S(1)} %get-tuple-element.42.refs_0_, bf16[48,7296]{1,0:T(8,128)(2,1)S(1)} %get-tuple-element.43.refs_1_, ...), custom_call_target="tpu_custom_call" | custom-call | flops 2113929216 | bytes 5505024 | tf_op jit(solution)/shard_map/experts/pallas_call | solution.py:316
  72.5 8.4 %collective-permute-done.16.refs_2_ = bf16[96,7168]{1,0:T(8,128)(2,1)S(1)} collective-permute-done((bf16[96,7168]{1,0:T(8,128)(2,1)S(1)}, bf16[96,7168]{1,0:T(8,128)(2,1)S(1)}, u32[]{:S(2)}, u32[]{:S(2)}) %collective-permute-start.16) | collective-permute-done | bytes 1376288 | tf_op jit(solution)/shard_map/ppermute | solution.py:44
  80.9 0.7 collective-permute-start.25
  81.7 0.4 add_convert_fusion
  82.1 1.3 %collective-permute-done.25.refs_2_ = bf16[48,7168]{1,0:T(8,128)(2,1)S(1)} collective-permute-done((bf16[48,7168]{1,0:T(8,128)(2,1)S(1)}, bf16[48,7168]{1,0:T(8,128)(2,1)S(1)}, u32[]{:S(2)}, u32[]{:S(2)}) %collective-permute-start.25) | collective-permute-done | bytes 688160 | tf_op jit(solution)/shard_map/ppermute | solution.py:48
  83.4 1.0 collective-permute-done.26.refs_3_
  84.4 0.3 join.1
  84.8 1.7 %collective-permute-start.29 = (bf16[24,7168]{1,0:T(8,128)(2,1)S(1)}, bf16[24,7168]{1,0:T(8,128)(2,1)S(1)}, u32[]{:S(2)}, u32[]{:S(2)}) collective-permute-start(bf16[24,7168]{1,0:T(8,128)(2,1)S(1)} %get-tuple-element.53), channel_id=1, source_target_pairs={{0,32},{1,33},{2,34},{3,35},{4,36},{5,37},{6,38},{7,39},{8,40},{9,... | collective-permute-start | bytes 1032200 | tf_op jit(solution)/shard_map/ppermute | solution.py:44
  86.5 1.0 collective-permute-start.28
  87.5 1.0 collective-permute-start.27
  88.5 0.4 add_convert_fusion.9
  88.9 2.0 %collective-permute-start.20 = (bf16[24,7168]{1,0:T(8,128)(2,1)S(1)}, bf16[24,7168]{1,0:T(8,128)(2,1)S(1)}, u32[]{:S(2)}, u32[]{:S(2)}) collective-permute-start(bf16[24,7168]{1,0:T(8,128)(2,1)S(1)} %get-tuple-element.55), channel_id=1, source_target_pairs={{0,32},{1,33},{2,34},{3,35},{4,36},{5,37},{6,38},{7,39},{8,40},{9,... | collective-permute-start | bytes 1032200 | tf_op jit(solution)/shard_map/ppermute | solution.py:44
  90.8 2.5 %collective-permute-start.19 = (bf16[24,7168]{1,0:T(8,128)(2,1)S(1)}, bf16[24,7168]{1,0:T(8,128)(2,1)S(1)}, u32[]{:S(2)}, u32[]{:S(2)}) collective-permute-start(bf16[24,7168]{1,0:T(8,128)(2,1)S(1)} %get-tuple-element.56), channel_id=1, source_target_pairs={{0,48},{1,49},{2,50},{3,51},{4,52},{5,53},{6,54},{7,55},{8,56},{9,... | collective-permute-start | bytes 1032200 | tf_op jit(solution)/shard_map/ppermute | solution.py:44
  93.4 0.3 collective-permute-done.29
  93.7 3.5 %collective-permute-done.28 = bf16[24,7168]{1,0:T(8,128)(2,1)S(1)} collective-permute-done((bf16[24,7168]{1,0:T(8,128)(2,1)S(1)}, bf16[24,7168]{1,0:T(8,128)(2,1)S(1)}, u32[]{:S(2)}, u32[]{:S(2)}) %collective-permute-start.28) | collective-permute-done | bytes 344096 | tf_op jit(solution)/shard_map/ppermute | solution.py:44
  97.3 0.2 add_convert_fusion.6
  97.5 1.9 %collective-permute-start.30 = (bf16[24,7168]{1,0:T(8,128)(2,1)S(1)}, bf16[24,7168]{1,0:T(8,128)(2,1)S(1)}, u32[]{:S(2)}, u32[]{:S(2)}) collective-permute-start(bf16[24,7168]{1,0:T(8,128)(2,1)S(1)} %add_convert_fusion.6), channel_id=1, source_target_pairs={{0,2},{1,3},{2,0},{3,1},{4,6},{5,7},{6,4},{7,5},{8,10},{9,11},{10,... | collective-permute-start | bytes 1032200 | tf_op jit(solution)/shard_map/ppermute | solution.py:44
  99.4 1.7 %collective-permute-done.20 = bf16[24,7168]{1,0:T(8,128)(2,1)S(1)} collective-permute-done((bf16[24,7168]{1,0:T(8,128)(2,1)S(1)}, bf16[24,7168]{1,0:T(8,128)(2,1)S(1)}, u32[]{:S(2)}, u32[]{:S(2)}) %collective-permute-start.20) | collective-permute-done | bytes 344096 | tf_op jit(solution)/shard_map/ppermute | solution.py:44
  101.1 6.2 %collective-permute-done.19 = bf16[24,7168]{1,0:T(8,128)(2,1)S(1)} collective-permute-done((bf16[24,7168]{1,0:T(8,128)(2,1)S(1)}, bf16[24,7168]{1,0:T(8,128)(2,1)S(1)}, u32[]{:S(2)}, u32[]{:S(2)}) %collective-permute-start.19) | collective-permute-done | bytes 344096 | tf_op jit(solution)/shard_map/ppermute | solution.py:44
  107.3 0.3 add_convert_fusion.5
  107.6 0.1 fusion
  107.7 2.6 %collective-permute-start.33 = (bf16[6,7168]{1,0:T(8,128)(2,1)S(1)}, bf16[6,7168]{1,0:T(8,128)(2,1)S(1)}, u32[]{:S(2)}, u32[]{:S(2)}) collective-permute-start(bf16[6,7168]{1,0:T(8,128)(2,1)S(1)} %get-tuple-element.62), channel_id=1, source_target_pairs={{0,8},{1,9},{2,10},{3,11},{4,12},{5,13},{6,14},{7,15},{8,0},{9,1},... | collective-permute-start | bytes 258056 | tf_op jit(solution)/shard_map/ppermute | solution.py:44
  110.3 2.9 %collective-permute-start.32 = (bf16[6,7168]{1,0:T(8,128)(2,1)S(1)}, bf16[6,7168]{1,0:T(8,128)(2,1)S(1)}, u32[]{:S(2)}, u32[]{:S(2)}) collective-permute-start(bf16[6,7168]{1,0:T(8,128)(2,1)S(1)} %get-tuple-element.63), channel_id=1, source_target_pairs={{0,12},{1,13},{2,14},{3,15},{4,0},{5,1},{6,2},{7,3},{8,4},{9,5},{1... | collective-permute-start | bytes 258056 | tf_op jit(solution)/shard_map/ppermute | solution.py:44
  113.3 0.1 collective-permute-start.31
  113.3 0.8 collective-permute-done.33
  114.1 3.2 %collective-permute-done.32 = bf16[6,7168]{1,0:T(8,128)(2,1)S(1)} collective-permute-done((bf16[6,7168]{1,0:T(8,128)(2,1)S(1)}, bf16[6,7168]{1,0:T(8,128)(2,1)S(1)}, u32[]{:S(2)}, u32[]{:S(2)}) %collective-permute-start.32) | collective-permute-done | bytes 86048 | tf_op jit(solution)/shard_map/ppermute | solution.py:44
  117.3 1.9 %collective-permute-done.31 = bf16[6,7168]{1,0:T(8,128)(2,1)S(1)} collective-permute-done((bf16[6,7168]{1,0:T(8,128)(2,1)S(1)}, bf16[6,7168]{1,0:T(8,128)(2,1)S(1)}, u32[]{:S(2)}, u32[]{:S(2)}) %collective-permute-start.31) | collective-permute-done | bytes 86048 | tf_op jit(solution)/shard_map/ppermute | solution.py:44
  119.3 0.7 reshape.11
  (39 shorter events, 0.5 us)
Async XLA Ops:
  1.8 6.6 %collective-permute-start = (bf16[6,7296]{1,0:T(8,128)(2,1)S(1)}, bf16[6,7296]{1,0:T(8,128)(2,1)S(1)}, u32[]{:S(2)}, u32[]{:S(2)}) collective-permute-start(bf16[6,7296]{1,0:T(8,128)(2,1)S(1)} %prepare.1.refs_0_), channel_id=1, source_target_pairs={{0,12},{1,13},{2,14},{3,15},{4,0},{5,1},{6,2},{7,3},{8,4},{9,5},{1... | collective-permute-start | bytes 262664 | tf_op jit(solution)/shard_map/ppermute | solution.py:44
  6.0 7.3 %collective-permute-start.1 = (bf16[6,7296]{1,0:T(8,128)(2,1)S(1)}, bf16[6,7296]{1,0:T(8,128)(2,1)S(1)}, u32[]{:S(2)}, u32[]{:S(2)}) collective-permute-start(bf16[6,7296]{1,0:T(8,128)(2,1)S(1)} %prepare.1.refs_0_), channel_id=1, source_target_pairs={{0,4},{1,5},{2,6},{3,7},{4,8},{5,9},{6,10},{7,11},{8,12},{9,13},{1... | collective-permute-start | bytes 262664 | tf_op jit(solution)/shard_map/ppermute | solution.py:44
  6.0 7.3 %collective-permute-start.2 = (bf16[6,7296]{1,0:T(8,128)(2,1)S(1)}, bf16[6,7296]{1,0:T(8,128)(2,1)S(1)}, u32[]{:S(2)}, u32[]{:S(2)}) collective-permute-start(bf16[6,7296]{1,0:T(8,128)(2,1)S(1)} %prepare.1.refs_0_), channel_id=1, source_target_pairs={{0,8},{1,9},{2,10},{3,11},{4,12},{5,13},{6,14},{7,15},{8,0},{9,1},... | collective-permute-start | bytes 262664 | tf_op jit(solution)/shard_map/ppermute | solution.py:44
  13.4 18.7 %copy-start.1 = (bf16[3,2,576]{2,1,0:T(2,128)(2,1)S(1)}, bf16[3,2,576]{2,1,0:T(2,128)(2,1)}, u32[]{:S(2)}) copy-start(bf16[3,2,576]{2,1,0:T(2,128)(2,1)} %param.20) | copy-start | bytes 20740
  13.4 18.7 %copy-start = (s32[2]{0:T(128)S(1)}, s32[2]{0:T(128)}, u32[]{:S(2)}) copy-start(s32[2]{0:T(128)} %length_ref.1) | copy-start | bytes 28
  13.4 8.0 %collective-permute-start.3 = (bf16[24,7296]{1,0:T(8,128)(2,1)S(1)}, bf16[24,7296]{1,0:T(8,128)(2,1)S(1)}, u32[]{:S(2)}, u32[]{:S(2)}) collective-permute-start(bf16[24,7296]{1,0:T(8,128)(2,1)S(1)} %stack.8.refs_0_), channel_id=1, source_target_pairs={{0,48},{1,49},{2,50},{3,51},{4,52},{5,53},{6,54},{7,55},{8,56},{9,... | collective-permute-start | bytes 1050632 | tf_op jit(solution)/shard_map/ppermute | solution.py:44
  16.5 12.3 %collective-permute-start.4 = (bf16[24,7296]{1,0:T(8,128)(2,1)S(1)}, bf16[24,7296]{1,0:T(8,128)(2,1)S(1)}, u32[]{:S(2)}, u32[]{:S(2)}) collective-permute-start(bf16[24,7296]{1,0:T(8,128)(2,1)S(1)} %stack.8.refs_0_), channel_id=1, source_target_pairs={{0,16},{1,17},{2,18},{3,19},{4,20},{5,21},{6,22},{7,23},{8,24},{9,... | collective-permute-start | bytes 1050632 | tf_op jit(solution)/shard_map/ppermute | solution.py:44
  16.5 12.3 %collective-permute-start.5 = (bf16[24,7296]{1,0:T(8,128)(2,1)S(1)}, bf16[24,7296]{1,0:T(8,128)(2,1)S(1)}, u32[]{:S(2)}, u32[]{:S(2)}) collective-permute-start(bf16[24,7296]{1,0:T(8,128)(2,1)S(1)} %stack.8.refs_0_), channel_id=1, source_target_pairs={{0,32},{1,33},{2,34},{3,35},{4,36},{5,37},{6,38},{7,39},{8,40},{9,... | collective-permute-start | bytes 1050632 | tf_op jit(solution)/shard_map/ppermute | solution.py:44
  21.4 19.1 %collective-permute-start.6 = (bf16[48,7296]{1,0:T(8,128)(2,1)S(1)}, bf16[48,7296]{1,0:T(8,128)(2,1)S(1)}, u32[]{:S(2)}, u32[]{:S(2)}) collective-permute-start(bf16[48,7296]{1,0:T(8,128)(2,1)S(1)} %stack.9.refs_0_), channel_id=1, source_target_pairs={{0,3},{1,0},{2,1},{3,2},{4,7},{5,4},{6,5},{7,6},{8,11},{9,8},{10,9... | collective-permute-start | bytes 2101256 | tf_op jit(solution)/shard_map/ppermute | solution.py:44
  24.2 16.2 %collective-permute-start.7 = (bf16[48,7296]{1,0:T(8,128)(2,1)S(1)}, bf16[48,7296]{1,0:T(8,128)(2,1)S(1)}, u32[]{:S(2)}, u32[]{:S(2)}) collective-permute-start(bf16[48,7296]{1,0:T(8,128)(2,1)S(1)} %stack.9.refs_0_), channel_id=1, source_target_pairs={{0,1},{1,2},{2,3},{3,0},{4,5},{5,6},{6,7},{7,4},{8,9},{9,10},{10,1... | collective-permute-start | bytes 2101256 | tf_op jit(solution)/shard_map/ppermute | solution.py:44
  28.8 15.9 %collective-permute-start.8 = (bf16[48,7296]{1,0:T(8,128)(2,1)S(1)}, bf16[48,7296]{1,0:T(8,128)(2,1)S(1)}, u32[]{:S(2)}, u32[]{:S(2)}) collective-permute-start(bf16[48,7296]{1,0:T(8,128)(2,1)S(1)} %stack.10.refs_1_), channel_id=1, source_target_pairs={{0,3},{1,0},{2,1},{3,2},{4,7},{5,4},{6,5},{7,6},{8,11},{9,8},{10,9... | collective-permute-start | bytes 2101256 | tf_op jit(solution)/shard_map/ppermute | solution.py:44
  32.1 12.7 %collective-permute-start.9 = (bf16[48,7296]{1,0:T(8,128)(2,1)S(1)}, bf16[48,7296]{1,0:T(8,128)(2,1)S(1)}, u32[]{:S(2)}, u32[]{:S(2)}) collective-permute-start(bf16[48,7296]{1,0:T(8,128)(2,1)S(1)} %stack.10.refs_1_), channel_id=1, source_target_pairs={{0,1},{1,2},{2,3},{3,0},{4,5},{5,6},{6,7},{7,4},{8,9},{9,10},{10,1... | collective-permute-start | bytes 2101256 | tf_op jit(solution)/shard_map/ppermute | solution.py:44
  44.9 3.3 %collective-permute-start.12 = (bf16[96,7296]{1,0:T(8,128)(2,1)S(1)}, bf16[96,7296]{1,0:T(8,128)(2,1)S(1)}, u32[]{:S(2)}, u32[]{:S(2)}) collective-permute-start(bf16[96,7296]{1,0:T(8,128)(2,1)S(1)} %stack.13), channel_id=1, source_target_pairs={{0,64},{64,0},{1,65},{65,1},{2,66},{66,2},{3,67},{67,3},{4,68},{68... | collective-permute-start | bytes 4202504 | tf_op jit(solution)/shard_map/ppermute | solution.py:48
  45.1 8.8 %collective-permute-start.11 = (bf16[96,7296]{1,0:T(8,128)(2,1)S(1)}, bf16[96,7296]{1,0:T(8,128)(2,1)S(1)}, u32[]{:S(2)}, u32[]{:S(2)}) collective-permute-start(bf16[96,7296]{1,0:T(8,128)(2,1)S(1)} %stack.12), channel_id=1, source_target_pairs={{0,64},{64,0},{1,65},{65,1},{2,66},{66,2},{3,67},{67,3},{4,68},{68... | collective-permute-start | bytes 4202504 | tf_op jit(solution)/shard_map/ppermute | solution.py:48
  45.6 12.2 %collective-permute-start.10 = (bf16[96,7296]{1,0:T(8,128)(2,1)S(1)}, bf16[96,7296]{1,0:T(8,128)(2,1)S(1)}, u32[]{:S(2)}, u32[]{:S(2)}) collective-permute-start(bf16[96,7296]{1,0:T(8,128)(2,1)S(1)} %get-tuple-element.31.refs_0_), channel_id=1, source_target_pairs={{0,64},{64,0},{1,65},{65,1},{2,66},{66,2},{3,67},{67,3},{4,68},{68... | collective-permute-start | bytes 4202504 | tf_op jit(solution)/shard_map/ppermute | solution.py:48
  50.2 10.3 %collective-permute-start.14 = (bf16[96,7168]{1,0:T(8,128)(2,1)S(1)}, bf16[96,7168]{1,0:T(8,128)(2,1)S(1)}, u32[]{:S(2)}, u32[]{:S(2)}) collective-permute-start(bf16[96,7168]{1,0:T(8,128)(2,1)S(1)} %experts.6.refs_4_), channel_id=1, source_target_pairs={{0,64},{64,0},{1,65},{65,1},{2,66},{66,2},{3,67},{67,3},{4,68},{68... | collective-permute-start | bytes 4128776 | tf_op jit(solution)/shard_map/ppermute | solution.py:48
  50.7 14.1 %collective-permute-start.21 = (bf16[48,7296]{1,0:T(8,128)(2,1)S(1)}, bf16[48,7296]{1,0:T(8,128)(2,1)S(1)}, u32[]{:S(2)}, u32[]{:S(2)}) collective-permute-start(bf16[48,7296]{1,0:T(8,128)(2,1)S(1)} %get-tuple-element.34.refs_0_), channel_id=1, source_target_pairs={{0,3},{1,0},{2,1},{3,2},{4,7},{5,4},{6,5},{7,6},{8,11},{9,8},{10,9... | collective-permute-start | bytes 2101256 | tf_op jit(solution)/shard_map/ppermute | solution.py:44
  53.9 12.3 %collective-permute-start.22 = (bf16[48,7296]{1,0:T(8,128)(2,1)S(1)}, bf16[48,7296]{1,0:T(8,128)(2,1)S(1)}, u32[]{:S(2)}, u32[]{:S(2)}) collective-permute-start(bf16[48,7296]{1,0:T(8,128)(2,1)S(1)} %get-tuple-element.33.refs_1_.refs_3_), channel_id=1, source_target_pairs={{0,1},{1,2},{2,3},{3,0},{4,5},{5,6},{6,7},{7,4},{8,9},{9,10},{10,1... | collective-permute-start | bytes 2101256 | tf_op jit(solution)/shard_map/ppermute | solution.py:44
  55.9 4.9 %collective-permute-start.15 = (bf16[96,7168]{1,0:T(8,128)(2,1)S(1)}, bf16[96,7168]{1,0:T(8,128)(2,1)S(1)}, u32[]{:S(2)}, u32[]{:S(2)}) collective-permute-start(bf16[96,7168]{1,0:T(8,128)(2,1)S(1)} %experts.7.refs_5_), channel_id=1, source_target_pairs={{0,64},{64,0},{1,65},{65,1},{2,66},{66,2},{3,67},{67,3},{4,68},{68... | collective-permute-start | bytes 4128776 | tf_op jit(solution)/shard_map/ppermute | solution.py:48
  60.4 12.1 %collective-permute-start.13 = (bf16[96,7168]{1,0:T(8,128)(2,1)S(1)}, bf16[96,7168]{1,0:T(8,128)(2,1)S(1)}, u32[]{:S(2)}, u32[]{:S(2)}) collective-permute-start(bf16[96,7168]{1,0:T(8,128)(2,1)S(1)} %get-tuple-element.38), channel_id=1, source_target_pairs={{0,64},{64,0},{1,65},{65,1},{2,66},{66,2},{3,67},{67,3},{4,68},{68... | collective-permute-start | bytes 4128776 | tf_op jit(solution)/shard_map/ppermute | solution.py:48
  61.3 19.6 %collective-permute-start.16 = (bf16[96,7168]{1,0:T(8,128)(2,1)S(1)}, bf16[96,7168]{1,0:T(8,128)(2,1)S(1)}, u32[]{:S(2)}, u32[]{:S(2)}) collective-permute-start(bf16[96,7168]{1,0:T(8,128)(2,1)S(1)} %stack.14), channel_id=1, source_target_pairs={{0,1},{1,2},{2,3},{3,0},{4,5},{5,6},{6,7},{7,4},{8,9},{9,10},{10,1... | collective-permute-start | bytes 4128776 | tf_op jit(solution)/shard_map/ppermute | solution.py:44
  61.5 19.5 %collective-permute-start.17 = (bf16[96,7168]{1,0:T(8,128)(2,1)S(1)}, bf16[96,7168]{1,0:T(8,128)(2,1)S(1)}, u32[]{:S(2)}, u32[]{:S(2)}) collective-permute-start(bf16[96,7168]{1,0:T(8,128)(2,1)S(1)} %stack.15), channel_id=1, source_target_pairs={{0,3},{1,0},{2,1},{3,2},{4,7},{5,4},{6,5},{7,6},{8,11},{9,8},{10,9... | collective-permute-start | bytes 4128776 | tf_op jit(solution)/shard_map/ppermute | solution.py:44
  66.2 2.8 %collective-permute-start.23 = (bf16[48,7296]{1,0:T(8,128)(2,1)S(1)}, bf16[48,7296]{1,0:T(8,128)(2,1)S(1)}, u32[]{:S(2)}, u32[]{:S(2)}) collective-permute-start(bf16[48,7296]{1,0:T(8,128)(2,1)S(1)} %get-tuple-element.42.refs_0_), channel_id=1, source_target_pairs={{0,64},{64,0},{1,65},{65,1},{2,66},{66,2},{3,67},{67,3},{4,68},{68... | collective-permute-start | bytes 2101256 | tf_op jit(solution)/shard_map/ppermute | solution.py:48
  67.2 2.8 %collective-permute-start.24 = (bf16[48,7296]{1,0:T(8,128)(2,1)S(1)}, bf16[48,7296]{1,0:T(8,128)(2,1)S(1)}, u32[]{:S(2)}, u32[]{:S(2)}) collective-permute-start(bf16[48,7296]{1,0:T(8,128)(2,1)S(1)} %get-tuple-element.43.refs_1_), channel_id=1, source_target_pairs={{0,64},{64,0},{1,65},{65,1},{2,66},{66,2},{3,67},{67,3},{4,68},{68... | collective-permute-start | bytes 2101256 | tf_op jit(solution)/shard_map/ppermute | solution.py:48
  80.9 2.5 %collective-permute-start.25 = (bf16[48,7168]{1,0:T(8,128)(2,1)S(1)}, bf16[48,7168]{1,0:T(8,128)(2,1)S(1)}, u32[]{:S(2)}, u32[]{:S(2)}) collective-permute-start(bf16[48,7168]{1,0:T(8,128)(2,1)S(1)} %get-tuple-element.48), channel_id=1, source_target_pairs={{0,64},{64,0},{1,65},{65,1},{2,66},{66,2},{3,67},{67,3},{4,68},{68... | collective-permute-start | bytes 2064392 | tf_op jit(solution)/shard_map/ppermute | solution.py:48
  81.7 2.8 %collective-permute-start.26 = (bf16[48,7168]{1,0:T(8,128)(2,1)S(1)}, bf16[48,7168]{1,0:T(8,128)(2,1)S(1)}, u32[]{:S(2)}, u32[]{:S(2)}) collective-permute-start(bf16[48,7168]{1,0:T(8,128)(2,1)S(1)} %get-tuple-element.49), channel_id=1, source_target_pairs={{0,64},{64,0},{1,65},{65,1},{2,66},{66,2},{3,67},{67,3},{4,68},{68... | collective-permute-start | bytes 2064392 | tf_op jit(solution)/shard_map/ppermute | solution.py:48
  84.8 8.9 %collective-permute-start.29 = (bf16[24,7168]{1,0:T(8,128)(2,1)S(1)}, bf16[24,7168]{1,0:T(8,128)(2,1)S(1)}, u32[]{:S(2)}, u32[]{:S(2)}) collective-permute-start(bf16[24,7168]{1,0:T(8,128)(2,1)S(1)} %get-tuple-element.53), channel_id=1, source_target_pairs={{0,32},{1,33},{2,34},{3,35},{4,36},{5,37},{6,38},{7,39},{8,40},{9,... | collective-permute-start | bytes 1032200 | tf_op jit(solution)/shard_map/ppermute | solution.py:44
  86.5 10.7 %collective-permute-start.28 = (bf16[24,7168]{1,0:T(8,128)(2,1)S(1)}, bf16[24,7168]{1,0:T(8,128)(2,1)S(1)}, u32[]{:S(2)}, u32[]{:S(2)}) collective-permute-start(bf16[24,7168]{1,0:T(8,128)(2,1)S(1)} %get-tuple-element.52), channel_id=1, source_target_pairs={{0,48},{1,49},{2,50},{3,51},{4,52},{5,53},{6,54},{7,55},{8,56},{9,... | collective-permute-start | bytes 1032200 | tf_op jit(solution)/shard_map/ppermute | solution.py:44
  87.5 9.8 %collective-permute-start.27 = (bf16[24,7168]{1,0:T(8,128)(2,1)S(1)}, bf16[24,7168]{1,0:T(8,128)(2,1)S(1)}, u32[]{:S(2)}, u32[]{:S(2)}) collective-permute-start(bf16[24,7168]{1,0:T(8,128)(2,1)S(1)} %get-tuple-element.51), channel_id=1, source_target_pairs={{0,16},{1,17},{2,18},{3,19},{4,20},{5,21},{6,22},{7,23},{8,24},{9,... | collective-permute-start | bytes 1032200 | tf_op jit(solution)/shard_map/ppermute | solution.py:44
  88.9 12.2 %collective-permute-start.20 = (bf16[24,7168]{1,0:T(8,128)(2,1)S(1)}, bf16[24,7168]{1,0:T(8,128)(2,1)S(1)}, u32[]{:S(2)}, u32[]{:S(2)}) collective-permute-start(bf16[24,7168]{1,0:T(8,128)(2,1)S(1)} %get-tuple-element.55), channel_id=1, source_target_pairs={{0,32},{1,33},{2,34},{3,35},{4,36},{5,37},{6,38},{7,39},{8,40},{9,... | collective-permute-start | bytes 1032200 | tf_op jit(solution)/shard_map/ppermute | solution.py:44
  90.8 16.5 %collective-permute-start.19 = (bf16[24,7168]{1,0:T(8,128)(2,1)S(1)}, bf16[24,7168]{1,0:T(8,128)(2,1)S(1)}, u32[]{:S(2)}, u32[]{:S(2)}) collective-permute-start(bf16[24,7168]{1,0:T(8,128)(2,1)S(1)} %get-tuple-element.56), channel_id=1, source_target_pairs={{0,48},{1,49},{2,50},{3,51},{4,52},{5,53},{6,54},{7,55},{8,56},{9,... | collective-permute-start | bytes 1032200 | tf_op jit(solution)/shard_map/ppermute | solution.py:44
  93.7 13.6 %collective-permute-start.18 = (bf16[24,7168]{1,0:T(8,128)(2,1)S(1)}, bf16[24,7168]{1,0:T(8,128)(2,1)S(1)}, u32[]{:S(2)}, u32[]{:S(2)}) collective-permute-start(bf16[24,7168]{1,0:T(8,128)(2,1)S(1)} %get-tuple-element.54), channel_id=1, source_target_pairs={{0,16},{1,17},{2,18},{3,19},{4,20},{5,21},{6,22},{7,23},{8,24},{9,... | collective-permute-start | bytes 1032200 | tf_op jit(solution)/shard_map/ppermute | solution.py:44
  97.5 9.9 %collective-permute-start.30 = (bf16[24,7168]{1,0:T(8,128)(2,1)S(1)}, bf16[24,7168]{1,0:T(8,128)(2,1)S(1)}, u32[]{:S(2)}, u32[]{:S(2)}) collective-permute-start(bf16[24,7168]{1,0:T(8,128)(2,1)S(1)} %add_convert_fusion.6), channel_id=1, source_target_pairs={{0,2},{1,3},{2,0},{3,1},{4,6},{5,7},{6,4},{7,5},{8,10},{9,11},{10,... | collective-permute-start | bytes 1032200 | tf_op jit(solution)/shard_map/ppermute | solution.py:44
  107.7 6.4 %collective-permute-start.33 = (bf16[6,7168]{1,0:T(8,128)(2,1)S(1)}, bf16[6,7168]{1,0:T(8,128)(2,1)S(1)}, u32[]{:S(2)}, u32[]{:S(2)}) collective-permute-start(bf16[6,7168]{1,0:T(8,128)(2,1)S(1)} %get-tuple-element.62), channel_id=1, source_target_pairs={{0,8},{1,9},{2,10},{3,11},{4,12},{5,13},{6,14},{7,15},{8,0},{9,1},... | collective-permute-start | bytes 258056 | tf_op jit(solution)/shard_map/ppermute | solution.py:44
  110.3 7.0 %collective-permute-start.32 = (bf16[6,7168]{1,0:T(8,128)(2,1)S(1)}, bf16[6,7168]{1,0:T(8,128)(2,1)S(1)}, u32[]{:S(2)}, u32[]{:S(2)}) collective-permute-start(bf16[6,7168]{1,0:T(8,128)(2,1)S(1)} %get-tuple-element.63), channel_id=1, source_target_pairs={{0,12},{1,13},{2,14},{3,15},{4,0},{5,1},{6,2},{7,3},{8,4},{9,5},{1... | collective-permute-start | bytes 258056 | tf_op jit(solution)/shard_map/ppermute | solution.py:44
  113.3 6.0 %collective-permute-start.31 = (bf16[6,7168]{1,0:T(8,128)(2,1)S(1)}, bf16[6,7168]{1,0:T(8,128)(2,1)S(1)}, u32[]{:S(2)}, u32[]{:S(2)}) collective-permute-start(bf16[6,7168]{1,0:T(8,128)(2,1)S(1)} %get-tuple-element.61), channel_id=1, source_target_pairs={{0,4},{1,5},{2,6},{3,7},{4,8},{5,9},{6,10},{7,11},{8,12},{9,13},{1... | collective-permute-start | bytes 258056 | tf_op jit(solution)/shard_map/ppermute | solution.py:44

commit v2 on v1

--- a/solution.py
+++ b/solution.py
@@ -16,7 +16,7 @@
 SIDE = 4
 GATE_LANES = 128
 SLOT_CHUNK = 512
-FEATURE_CHUNK = 1792
+FEATURE_CHUNK = 3584
 SMALL_VMEM = 4 * 1024 * 1024
 ATTEND_VMEM = 16 * 1024 * 1024
 JOIN_VMEM = 12 * 1024 * 1024

time: 120 us -> 120 us (level)
  no operation moved by 1% of the time
where the time goes in v2:
time: 120 us
  waiting for transfers between devices  45.3 us (38%)
  starting transfers between devices  45 us (38%)
  Pallas kernels  26.1 us (22%)
  other arithmetic  1.96 us (2%)
    ppermute x24, waiting for transfers between devices, shift(): return lax.ppermute(block, AXES, shifted_pairs(axis_of_core, distance))  40.2 us
    ppermute x24, starting transfers between devices, shift(): return lax.ppermute(block, AXES, shifted_pairs(axis_of_core, distance))  39.9 us
    pallas_call x5, Pallas kernels, expert_call(): pl.pallas_call(functools.partial(expert_body, count=count), out_shape=[ja...  11.4 us
    pallas_call x1, Pallas kernels, attend(): pl.pallas_call(attend_body, out_shape=jax.ShapeDtypeStruct((steps, reques...  8.25 us
    ppermute x10, starting transfers between devices, other_core(): return lax.ppermute(block, 'c', [(0, 1), (1, 0)])  5.13 us
    ppermute x10, waiting for transfers between devices, other_core(): return lax.ppermute(block, 'c', [(0, 1), (1, 0)])  5.12 us
    pallas_call x1, Pallas kernels, resident(): pl.pallas_call(functools.partial(resident_body, count=count), out_shape=[...  4.23 us
  transfers between devices with their start and end apart: 34, of which 18 were waited for; matrix products, arithmetic and copies ran while one was open for 1% of the time, Pallas kernels for 20%

profile of v2, /device:TPU:0, one launch (start us, length us, event | category | flops | bytes accessed | tf_op | source)
XLA Modules:
  0.0 120.0 jit_solution(11770762573408924188)
XLA Ops:
  0.6 1.2 prepare.1.refs_0_
  1.8 4.2 %collective-permute-start = (bf16[6,7296]{1,0:T(8,128)(2,1)S(1)}, bf16[6,7296]{1,0:T(8,128)(2,1)S(1)}, u32[]{:S(2)}, u32[]{:S(2)}) collective-permute-start(bf16[6,7296]{1,0:T(8,128)(2,1)S(1)} %prepare.1.refs_0_), channel_id=1, source_target_pairs={{0,12},{1,13},{2,14},{3,15},{4,0},{5,1},{6,2},{7,3},{8,4},{9,5},{1... | collective-permute-start | bytes 262664 | tf_op jit(solution)/shard_map/ppermute | solution.py:44
  6.0 1.9 %collective-permute-start.2 = (bf16[6,7296]{1,0:T(8,128)(2,1)S(1)}, bf16[6,7296]{1,0:T(8,128)(2,1)S(1)}, u32[]{:S(2)}, u32[]{:S(2)}) collective-permute-start(bf16[6,7296]{1,0:T(8,128)(2,1)S(1)} %prepare.1.refs_0_), channel_id=1, source_target_pairs={{0,8},{1,9},{2,10},{3,11},{4,12},{5,13},{6,14},{7,15},{8,0},{9,1},... | collective-permute-start | bytes 262664 | tf_op jit(solution)/shard_map/ppermute | solution.py:44
  7.9 0.5 collective-permute-done.refs_1_
  8.4 4.9 %collective-permute-done.1.refs_2_ = bf16[6,7296]{1,0:T(8,128)(2,1)S(1)} collective-permute-done((bf16[6,7296]{1,0:T(8,128)(2,1)S(1)}, bf16[6,7296]{1,0:T(8,128)(2,1)S(1)}, u32[]{:S(2)}, u32[]{:S(2)}) %collective-permute-start.1) | collective-permute-done | bytes 87584 | tf_op jit(solution)/shard_map/ppermute | solution.py:44
  13.4 3.1 %collective-permute-start.3 = (bf16[24,7296]{1,0:T(8,128)(2,1)S(1)}, bf16[24,7296]{1,0:T(8,128)(2,1)S(1)}, u32[]{:S(2)}, u32[]{:S(2)}) collective-permute-start(bf16[24,7296]{1,0:T(8,128)(2,1)S(1)} %stack.8.refs_0_), channel_id=1, source_target_pairs={{0,48},{1,49},{2,50},{3,51},{4,52},{5,53},{6,54},{7,55},{8,56},{9,... | collective-permute-start | bytes 1050632 | tf_op jit(solution)/shard_map/ppermute | solution.py:44
  16.5 2.2 %collective-permute-start.5 = (bf16[24,7296]{1,0:T(8,128)(2,1)S(1)}, bf16[24,7296]{1,0:T(8,128)(2,1)S(1)}, u32[]{:S(2)}, u32[]{:S(2)}) collective-permute-start(bf16[24,7296]{1,0:T(8,128)(2,1)S(1)} %stack.8.refs_0_), channel_id=1, source_target_pairs={{0,32},{1,33},{2,34},{3,35},{4,36},{5,37},{6,38},{7,39},{8,40},{9,... | collective-permute-start | bytes 1050632 | tf_op jit(solution)/shard_map/ppermute | solution.py:44
  18.7 2.7 %collective-permute-done.3.refs_1_ = bf16[24,7296]{1,0:T(8,128)(2,1)S(1)} collective-permute-done((bf16[24,7296]{1,0:T(8,128)(2,1)S(1)}, bf16[24,7296]{1,0:T(8,128)(2,1)S(1)}, u32[]{:S(2)}, u32[]{:S(2)}) %collective-permute-start.3) | collective-permute-done | bytes 350240 | tf_op jit(solution)/shard_map/ppermute | solution.py:44
  21.4 2.8 %collective-permute-start.6 = (bf16[48,7296]{1,0:T(8,128)(2,1)S(1)}, bf16[48,7296]{1,0:T(8,128)(2,1)S(1)}, u32[]{:S(2)}, u32[]{:S(2)}) collective-permute-start(bf16[48,7296]{1,0:T(8,128)(2,1)S(1)} %stack.9.refs_0_), channel_id=1, source_target_pairs={{0,3},{1,0},{2,1},{3,2},{4,7},{5,4},{6,5},{7,6},{8,11},{9,8},{10,9... | collective-permute-start | bytes 2101256 | tf_op jit(solution)/shard_map/ppermute | solution.py:44
  24.2 4.5 %collective-permute-done.4.refs_0_ = bf16[24,7296]{1,0:T(8,128)(2,1)S(1)} collective-permute-done((bf16[24,7296]{1,0:T(8,128)(2,1)S(1)}, bf16[24,7296]{1,0:T(8,128)(2,1)S(1)}, u32[]{:S(2)}, u32[]{:S(2)}) %collective-permute-start.4) | collective-permute-done | bytes 350240 | tf_op jit(solution)/shard_map/ppermute | solution.py:44
  28.8 3.3 %collective-permute-start.8 = (bf16[48,7296]{1,0:T(8,128)(2,1)S(1)}, bf16[48,7296]{1,0:T(8,128)(2,1)S(1)}, u32[]{:S(2)}, u32[]{:S(2)}) collective-permute-start(bf16[48,7296]{1,0:T(8,128)(2,1)S(1)} %stack.10.refs_1_), channel_id=1, source_target_pairs={{0,3},{1,0},{2,1},{3,2},{4,7},{5,4},{6,5},{7,6},{8,11},{9,8},{10,9... | collective-permute-start | bytes 2101256 | tf_op jit(solution)/shard_map/ppermute | solution.py:44
  32.1 8.3 %attend.1.refs_3_ = bf16[3,2,128,512]{3,2,1,0:T(8,128)(2,1)} custom-call(s32[2]{0:T(128)S(1)} %copy-done, bf16[3,2,576,128]{3,2,1,0:T(8,128)(2,1)} %bitcast.9, bf16[2,576,2048]{2,1,0:T(8,128)(2,1)} %bitcast.8, bf16[2,16,576]{2,1,0:T(8,128)(2,1)S(1)} %pad.4.fresh_ref), custom_call_target="tpu_custom_call" | custom-call | flops 3422552064 | bytes 6389760 | tf_op jit(solution)/shard_map/attend/pallas_call | solution.py:191
  40.4 0.1 stack.11.refs_0_
  40.5 4.2 %resident.1 = (bf16[7168,256]{1,0:T(8,128)(2,1)S(1)}, bf16[7168,256]{1,0:T(8,128)(2,1)S(1)}, bf16[256,7168]{1,0:T(8,128)(2,1)S(1)}) custom-call(bf16[7168,256]{1,0:T(8,128)(2,1)} %refs_0_.1, bf16[7168,256]{1,0:T(8,128)(2,1)} %refs_1_.1, bf16[256,7168]{1,0:T(8,128)(2,1)} %refs_2_.1, bf16[3,2,128,512]{3,2,1,0:T(8,128)(2,1)} %attend.1.refs_3_, ...), custom_call_target="tpu_custom_call" | custom-call | tf_op jit(solution)/shard_map/resident/pallas_call | solution.py:264
  44.8 0.1 stack.13
  44.9 0.1 collective-permute-start.12
  45.0 0.1 stack.12
  45.1 0.6 collective-permute-start.11
  45.6 0.1 collective-permute-start.10
  45.7 2.5 %experts.5 = (bf16[48,7168]{1,0:T(8,128)(2,1)S(1)}, bf16[48,7168]{1,0:T(8,128)(2,1)S(1)}, bf16[48,7168]{1,0:T(8,128)(2,1)S(1)}, bf16[48,7168]{1,0:T(8,128)(2,1)S(1)}) custom-call(bf16[48,7296]{1,0:T(8,128)(2,1)S(1)} %get-tuple-element.34.refs_0_, bf16[48,7296]{1,0:T(8,128)(2,1)S(1)} %get-tuple-element.35.refs_1_, ...), custom_call_target="tpu_custom_call" | custom-call | flops 2113929216 | bytes 5505024 | tf_op jit(solution)/shard_map/experts/pallas_call | solution.py:316
  48.2 2.0 %experts.6.refs_4_ = bf16[96,7168]{1,0:T(8,128)(2,1)S(1)} custom-call(bf16[96,7296]{1,0:T(8,128)(2,1)S(1)} %collective-permute-done.12.refs_0_, bf16[7168,256]{1,0:T(8,128)(2,1)S(1)} %get-tuple-element.28.refs_5_.refs_4_.refs_1_.refs_2_, bf16[7168,256]{1,0:T(8,128)(2,1)S(1)} %get-tuple-element.29.refs_6_.refs_5_.refs_2_.refs_3_, ...), custom_call_target="tpu_custom_call" | custom-call | flops 1056964608 | bytes 2752512 | tf_op jit(solution)/shard_map/experts/pallas_call | solution.py:316
  50.2 0.5 collective-permute-start.14
  50.7 3.2 %collective-permute-start.21 = (bf16[48,7296]{1,0:T(8,128)(2,1)S(1)}, bf16[48,7296]{1,0:T(8,128)(2,1)S(1)}, u32[]{:S(2)}, u32[]{:S(2)}) collective-permute-start(bf16[48,7296]{1,0:T(8,128)(2,1)S(1)} %get-tuple-element.34.refs_0_), channel_id=1, source_target_pairs={{0,3},{1,0},{2,1},{3,2},{4,7},{5,4},{6,5},{7,6},{8,11},{9,8},{10,9... | collective-permute-start | bytes 2101256 | tf_op jit(solution)/shard_map/ppermute | solution.py:44
  53.9 2.0 %experts.7.refs_5_ = bf16[96,7168]{1,0:T(8,128)(2,1)S(1)} custom-call(bf16[96,7296]{1,0:T(8,128)(2,1)S(1)} %collective-permute-done.11.refs_0_, bf16[7168,256]{1,0:T(8,128)(2,1)S(1)} %get-tuple-element.28.refs_5_.refs_4_.refs_1_.refs_2_, bf16[7168,256]{1,0:T(8,128)(2,1)S(1)} %get-tuple-element.29.refs_6_.refs_5_.refs_2_.refs_3_, ...), custom_call_target="tpu_custom_call" | custom-call | flops 1056964608 | bytes 2752512 | tf_op jit(solution)/shard_map/experts/pallas_call | solution.py:316
  55.9 1.9 %collective-permute-start.15 = (bf16[96,7168]{1,0:T(8,128)(2,1)S(1)}, bf16[96,7168]{1,0:T(8,128)(2,1)S(1)}, u32[]{:S(2)}, u32[]{:S(2)}) collective-permute-start(bf16[96,7168]{1,0:T(8,128)(2,1)S(1)} %experts.7.refs_5_), channel_id=1, source_target_pairs={{0,64},{64,0},{1,65},{65,1},{2,66},{66,2},{3,67},{67,3},{4,68},{68... | collective-permute-start | bytes 4128776 | tf_op jit(solution)/shard_map/ppermute | solution.py:48
  57.9 2.5 %experts.8 = (bf16[96,7168]{1,0:T(8,128)(2,1)S(1)}, bf16[96,7168]{1,0:T(8,128)(2,1)S(1)}) custom-call(bf16[96,7296]{1,0:T(8,128)(2,1)S(1)} %get-tuple-element.31.refs_0_, bf16[96,7296]{1,0:T(8,128)(2,1)S(1)} %collective-permute-done.10.refs_1_, bf16[7168,256]{1,0:T(8,128)(2,1)S(1)} %get-tuple-element.28.refs_5_.refs_4_.refs_1_.refs_2_, ...), custom_call_target="tpu_custom_call" | custom-call | flops 2113929216 | bytes 5505024 | tf_op jit(solution)/shard_map/experts/pallas_call | solution.py:316
  60.4 0.1 collective-permute-start.13
  60.5 0.4 add_convert_fusion.2
  60.8 0.3 add_convert_fusion.1
  61.2 0.1 stack.14
  61.4 0.1 stack.15
  61.5 3.3 %collective-permute-start.17 = (bf16[96,7168]{1,0:T(8,128)(2,1)S(1)}, bf16[96,7168]{1,0:T(8,128)(2,1)S(1)}, u32[]{:S(2)}, u32[]{:S(2)}) collective-permute-start(bf16[96,7168]{1,0:T(8,128)(2,1)S(1)} %stack.15), channel_id=1, source_target_pairs={{0,3},{1,0},{2,1},{3,2},{4,7},{5,4},{6,5},{7,6},{8,11},{9,8},{10,9... | collective-permute-start | bytes 4128776 | tf_op jit(solution)/shard_map/ppermute | solution.py:44
  64.8 1.4 %collective-permute-done.22.refs_1_ = bf16[48,7296]{1,0:T(8,128)(2,1)S(1)} collective-permute-done((bf16[48,7296]{1,0:T(8,128)(2,1)S(1)}, bf16[48,7296]{1,0:T(8,128)(2,1)S(1)}, u32[]{:S(2)}, u32[]{:S(2)}) %collective-permute-start.22) | collective-permute-done | bytes 700448 | tf_op jit(solution)/shard_map/ppermute | solution.py:44
  66.2 1.0 collective-permute-start.23
  67.2 1.8 %collective-permute-done.23.refs_2_ = bf16[48,7296]{1,0:T(8,128)(2,1)S(1)} collective-permute-done((bf16[48,7296]{1,0:T(8,128)(2,1)S(1)}, bf16[48,7296]{1,0:T(8,128)(2,1)S(1)}, u32[]{:S(2)}, u32[]{:S(2)}) %collective-permute-start.23) | collective-permute-done | bytes 700448 | tf_op jit(solution)/shard_map/ppermute | solution.py:48
  69.0 1.0 collective-permute-done.24.refs_3_
  70.0 2.5 %experts.9 = (bf16[48,7168]{1,0:T(8,128)(2,1)S(1)}, bf16[48,7168]{1,0:T(8,128)(2,1)S(1)}, bf16[48,7168]{1,0:T(8,128)(2,1)S(1)}, bf16[48,7168]{1,0:T(8,128)(2,1)S(1)}) custom-call(bf16[48,7296]{1,0:T(8,128)(2,1)S(1)} %get-tuple-element.42.refs_0_, bf16[48,7296]{1,0:T(8,128)(2,1)S(1)} %get-tuple-element.43.refs_1_, ...), custom_call_target="tpu_custom_call" | custom-call | flops 2113929216 | bytes 5505024 | tf_op jit(solution)/shard_map/experts/pallas_call | solution.py:316
  72.5 8.4 %collective-permute-done.16.refs_2_ = bf16[96,7168]{1,0:T(8,128)(2,1)S(1)} collective-permute-done((bf16[96,7168]{1,0:T(8,128)(2,1)S(1)}, bf16[96,7168]{1,0:T(8,128)(2,1)S(1)}, u32[]{:S(2)}, u32[]{:S(2)}) %collective-permute-start.16) | collective-permute-done | bytes 1376288 | tf_op jit(solution)/shard_map/ppermute | solution.py:44
  80.9 0.7 collective-permute-start.25
  81.7 0.4 add_convert_fusion
  82.1 1.3 %collective-permute-done.25.refs_2_ = bf16[48,7168]{1,0:T(8,128)(2,1)S(1)} collective-permute-done((bf16[48,7168]{1,0:T(8,128)(2,1)S(1)}, bf16[48,7168]{1,0:T(8,128)(2,1)S(1)}, u32[]{:S(2)}, u32[]{:S(2)}) %collective-permute-start.25) | collective-permute-done | bytes 688160 | tf_op jit(solution)/shard_map/ppermute | solution.py:48
  83.4 1.0 collective-permute-done.26.refs_3_
  84.4 0.3 join.1
  84.8 1.7 %collective-permute-start.29 = (bf16[24,7168]{1,0:T(8,128)(2,1)S(1)}, bf16[24,7168]{1,0:T(8,128)(2,1)S(1)}, u32[]{:S(2)}, u32[]{:S(2)}) collective-permute-start(bf16[24,7168]{1,0:T(8,128)(2,1)S(1)} %get-tuple-element.53), channel_id=1, source_target_pairs={{0,32},{1,33},{2,34},{3,35},{4,36},{5,37},{6,38},{7,39},{8,40},{9,... | collective-permute-start | bytes 1032200 | tf_op jit(solution)/shard_map/ppermute | solution.py:44
  86.5 1.0 collective-permute-start.28
  87.5 1.0 collective-permute-start.27
  88.5 0.4 add_convert_fusion.9
  88.9 2.0 %collective-permute-start.20 = (bf16[24,7168]{1,0:T(8,128)(2,1)S(1)}, bf16[24,7168]{1,0:T(8,128)(2,1)S(1)}, u32[]{:S(2)}, u32[]{:S(2)}) collective-permute-start(bf16[24,7168]{1,0:T(8,128)(2,1)S(1)} %get-tuple-element.55), channel_id=1, source_target_pairs={{0,32},{1,33},{2,34},{3,35},{4,36},{5,37},{6,38},{7,39},{8,40},{9,... | collective-permute-start | bytes 1032200 | tf_op jit(solution)/shard_map/ppermute | solution.py:44
  90.8 2.6 %collective-permute-start.19 = (bf16[24,7168]{1,0:T(8,128)(2,1)S(1)}, bf16[24,7168]{1,0:T(8,128)(2,1)S(1)}, u32[]{:S(2)}, u32[]{:S(2)}) collective-permute-start(bf16[24,7168]{1,0:T(8,128)(2,1)S(1)} %get-tuple-element.56), channel_id=1, source_target_pairs={{0,48},{1,49},{2,50},{3,51},{4,52},{5,53},{6,54},{7,55},{8,56},{9,... | collective-permute-start | bytes 1032200 | tf_op jit(solution)/shard_map/ppermute | solution.py:44
  93.4 0.3 collective-permute-done.29
  93.7 3.5 %collective-permute-done.28 = bf16[24,7168]{1,0:T(8,128)(2,1)S(1)} collective-permute-done((bf16[24,7168]{1,0:T(8,128)(2,1)S(1)}, bf16[24,7168]{1,0:T(8,128)(2,1)S(1)}, u32[]{:S(2)}, u32[]{:S(2)}) %collective-permute-start.28) | collective-permute-done | bytes 344096 | tf_op jit(solution)/shard_map/ppermute | solution.py:44
  97.3 0.2 add_convert_fusion.6
  97.4 1.9 %collective-permute-start.30 = (bf16[24,7168]{1,0:T(8,128)(2,1)S(1)}, bf16[24,7168]{1,0:T(8,128)(2,1)S(1)}, u32[]{:S(2)}, u32[]{:S(2)}) collective-permute-start(bf16[24,7168]{1,0:T(8,128)(2,1)S(1)} %add_convert_fusion.6), channel_id=1, source_target_pairs={{0,2},{1,3},{2,0},{3,1},{4,6},{5,7},{6,4},{7,5},{8,10},{9,11},{10,... | collective-permute-start | bytes 1032200 | tf_op jit(solution)/shard_map/ppermute | solution.py:44
  99.4 1.7 %collective-permute-done.20 = bf16[24,7168]{1,0:T(8,128)(2,1)S(1)} collective-permute-done((bf16[24,7168]{1,0:T(8,128)(2,1)S(1)}, bf16[24,7168]{1,0:T(8,128)(2,1)S(1)}, u32[]{:S(2)}, u32[]{:S(2)}) %collective-permute-start.20) | collective-permute-done | bytes 344096 | tf_op jit(solution)/shard_map/ppermute | solution.py:44
  101.1 6.2 %collective-permute-done.19 = bf16[24,7168]{1,0:T(8,128)(2,1)S(1)} collective-permute-done((bf16[24,7168]{1,0:T(8,128)(2,1)S(1)}, bf16[24,7168]{1,0:T(8,128)(2,1)S(1)}, u32[]{:S(2)}, u32[]{:S(2)}) %collective-permute-start.19) | collective-permute-done | bytes 344096 | tf_op jit(solution)/shard_map/ppermute | solution.py:44
  107.3 0.3 add_convert_fusion.5
  107.6 0.1 fusion
  107.7 2.6 %collective-permute-start.33 = (bf16[6,7168]{1,0:T(8,128)(2,1)S(1)}, bf16[6,7168]{1,0:T(8,128)(2,1)S(1)}, u32[]{:S(2)}, u32[]{:S(2)}) collective-permute-start(bf16[6,7168]{1,0:T(8,128)(2,1)S(1)} %get-tuple-element.62), channel_id=1, source_target_pairs={{0,8},{1,9},{2,10},{3,11},{4,12},{5,13},{6,14},{7,15},{8,0},{9,1},... | collective-permute-start | bytes 258056 | tf_op jit(solution)/shard_map/ppermute | solution.py:44
  110.3 2.9 %collective-permute-start.32 = (bf16[6,7168]{1,0:T(8,128)(2,1)S(1)}, bf16[6,7168]{1,0:T(8,128)(2,1)S(1)}, u32[]{:S(2)}, u32[]{:S(2)}) collective-permute-start(bf16[6,7168]{1,0:T(8,128)(2,1)S(1)} %get-tuple-element.63), channel_id=1, source_target_pairs={{0,12},{1,13},{2,14},{3,15},{4,0},{5,1},{6,2},{7,3},{8,4},{9,5},{1... | collective-permute-start | bytes 258056 | tf_op jit(solution)/shard_map/ppermute | solution.py:44
  113.3 0.1 collective-permute-start.31
  113.3 0.8 collective-permute-done.33
  114.1 3.2 %collective-permute-done.32 = bf16[6,7168]{1,0:T(8,128)(2,1)S(1)} collective-permute-done((bf16[6,7168]{1,0:T(8,128)(2,1)S(1)}, bf16[6,7168]{1,0:T(8,128)(2,1)S(1)}, u32[]{:S(2)}, u32[]{:S(2)}) %collective-permute-start.32) | collective-permute-done | bytes 86048 | tf_op jit(solution)/shard_map/ppermute | solution.py:44
  117.3 1.9 %collective-permute-done.31 = bf16[6,7168]{1,0:T(8,128)(2,1)S(1)} collective-permute-done((bf16[6,7168]{1,0:T(8,128)(2,1)S(1)}, bf16[6,7168]{1,0:T(8,128)(2,1)S(1)}, u32[]{:S(2)}, u32[]{:S(2)}) %collective-permute-start.31) | collective-permute-done | bytes 86048 | tf_op jit(solution)/shard_map/ppermute | solution.py:44
  119.3 0.7 reshape.11
  (39 shorter events, 0.5 us)
Async XLA Ops:
  1.8 6.6 %collective-permute-start = (bf16[6,7296]{1,0:T(8,128)(2,1)S(1)}, bf16[6,7296]{1,0:T(8,128)(2,1)S(1)}, u32[]{:S(2)}, u32[]{:S(2)}) collective-permute-start(bf16[6,7296]{1,0:T(8,128)(2,1)S(1)} %prepare.1.refs_0_), channel_id=1, source_target_pairs={{0,12},{1,13},{2,14},{3,15},{4,0},{5,1},{6,2},{7,3},{8,4},{9,5},{1... | collective-permute-start | bytes 262664 | tf_op jit(solution)/shard_map/ppermute | solution.py:44
  6.0 7.3 %collective-permute-start.1 = (bf16[6,7296]{1,0:T(8,128)(2,1)S(1)}, bf16[6,7296]{1,0:T(8,128)(2,1)S(1)}, u32[]{:S(2)}, u32[]{:S(2)}) collective-permute-start(bf16[6,7296]{1,0:T(8,128)(2,1)S(1)} %prepare.1.refs_0_), channel_id=1, source_target_pairs={{0,4},{1,5},{2,6},{3,7},{4,8},{5,9},{6,10},{7,11},{8,12},{9,13},{1... | collective-permute-start | bytes 262664 | tf_op jit(solution)/shard_map/ppermute | solution.py:44
  6.0 7.3 %collective-permute-start.2 = (bf16[6,7296]{1,0:T(8,128)(2,1)S(1)}, bf16[6,7296]{1,0:T(8,128)(2,1)S(1)}, u32[]{:S(2)}, u32[]{:S(2)}) collective-permute-start(bf16[6,7296]{1,0:T(8,128)(2,1)S(1)} %prepare.1.refs_0_), channel_id=1, source_target_pairs={{0,8},{1,9},{2,10},{3,11},{4,12},{5,13},{6,14},{7,15},{8,0},{9,1},... | collective-permute-start | bytes 262664 | tf_op jit(solution)/shard_map/ppermute | solution.py:44
  13.4 18.7 %copy-start.1 = (bf16[3,2,576]{2,1,0:T(2,128)(2,1)S(1)}, bf16[3,2,576]{2,1,0:T(2,128)(2,1)}, u32[]{:S(2)}) copy-start(bf16[3,2,576]{2,1,0:T(2,128)(2,1)} %param.20) | copy-start | bytes 20740
  13.4 18.7 %copy-start = (s32[2]{0:T(128)S(1)}, s32[2]{0:T(128)}, u32[]{:S(2)}) copy-start(s32[2]{0:T(128)} %length_ref.1) | copy-start | bytes 28
  13.4 8.0 %collective-permute-start.3 = (bf16[24,7296]{1,0:T(8,128)(2,1)S(1)}, bf16[24,7296]{1,0:T(8,128)(2,1)S(1)}, u32[]{:S(2)}, u32[]{:S(2)}) collective-permute-start(bf16[24,7296]{1,0:T(8,128)(2,1)S(1)} %stack.8.refs_0_), channel_id=1, source_target_pairs={{0,48},{1,49},{2,50},{3,51},{4,52},{5,53},{6,54},{7,55},{8,56},{9,... | collective-permute-start | bytes 1050632 | tf_op jit(solution)/shard_map/ppermute | solution.py:44
  16.5 12.3 %collective-permute-start.4 = (bf16[24,7296]{1,0:T(8,128)(2,1)S(1)}, bf16[24,7296]{1,0:T(8,128)(2,1)S(1)}, u32[]{:S(2)}, u32[]{:S(2)}) collective-permute-start(bf16[24,7296]{1,0:T(8,128)(2,1)S(1)} %stack.8.refs_0_), channel_id=1, source_target_pairs={{0,16},{1,17},{2,18},{3,19},{4,20},{5,21},{6,22},{7,23},{8,24},{9,... | collective-permute-start | bytes 1050632 | tf_op jit(solution)/shard_map/ppermute | solution.py:44
  16.5 12.3 %collective-permute-start.5 = (bf16[24,7296]{1,0:T(8,128)(2,1)S(1)}, bf16[24,7296]{1,0:T(8,128)(2,1)S(1)}, u32[]{:S(2)}, u32[]{:S(2)}) collective-permute-start(bf16[24,7296]{1,0:T(8,128)(2,1)S(1)} %stack.8.refs_0_), channel_id=1, source_target_pairs={{0,32},{1,33},{2,34},{3,35},{4,36},{5,37},{6,38},{7,39},{8,40},{9,... | collective-permute-start | bytes 1050632 | tf_op jit(solution)/shard_map/ppermute | solution.py:44
  21.4 19.1 %collective-permute-start.6 = (bf16[48,7296]{1,0:T(8,128)(2,1)S(1)}, bf16[48,7296]{1,0:T(8,128)(2,1)S(1)}, u32[]{:S(2)}, u32[]{:S(2)}) collective-permute-start(bf16[48,7296]{1,0:T(8,128)(2,1)S(1)} %stack.9.refs_0_), channel_id=1, source_target_pairs={{0,3},{1,0},{2,1},{3,2},{4,7},{5,4},{6,5},{7,6},{8,11},{9,8},{10,9... | collective-permute-start | bytes 2101256 | tf_op jit(solution)/shard_map/ppermute | solution.py:44
  24.2 16.2 %collective-permute-start.7 = (bf16[48,7296]{1,0:T(8,128)(2,1)S(1)}, bf16[48,7296]{1,0:T(8,128)(2,1)S(1)}, u32[]{:S(2)}, u32[]{:S(2)}) collective-permute-start(bf16[48,7296]{1,0:T(8,128)(2,1)S(1)} %stack.9.refs_0_), channel_id=1, source_target_pairs={{0,1},{1,2},{2,3},{3,0},{4,5},{5,6},{6,7},{7,4},{8,9},{9,10},{10,1... | collective-permute-start | bytes 2101256 | tf_op jit(solution)/shard_map/ppermute | solution.py:44
  28.8 15.9 %collective-permute-start.8 = (bf16[48,7296]{1,0:T(8,128)(2,1)S(1)}, bf16[48,7296]{1,0:T(8,128)(2,1)S(1)}, u32[]{:S(2)}, u32[]{:S(2)}) collective-permute-start(bf16[48,7296]{1,0:T(8,128)(2,1)S(1)} %stack.10.refs_1_), channel_id=1, source_target_pairs={{0,3},{1,0},{2,1},{3,2},{4,7},{5,4},{6,5},{7,6},{8,11},{9,8},{10,9... | collective-permute-start | bytes 2101256 | tf_op jit(solution)/shard_map/ppermute | solution.py:44
  32.1 12.7 %collective-permute-start.9 = (bf16[48,7296]{1,0:T(8,128)(2,1)S(1)}, bf16[48,7296]{1,0:T(8,128)(2,1)S(1)}, u32[]{:S(2)}, u32[]{:S(2)}) collective-permute-start(bf16[48,7296]{1,0:T(8,128)(2,1)S(1)} %stack.10.refs_1_), channel_id=1, source_target_pairs={{0,1},{1,2},{2,3},{3,0},{4,5},{5,6},{6,7},{7,4},{8,9},{9,10},{10,1... | collective-permute-start | bytes 2101256 | tf_op jit(solution)/shard_map/ppermute | solution.py:44
  44.9 3.3 %collective-permute-start.12 = (bf16[96,7296]{1,0:T(8,128)(2,1)S(1)}, bf16[96,7296]{1,0:T(8,128)(2,1)S(1)}, u32[]{:S(2)}, u32[]{:S(2)}) collective-permute-start(bf16[96,7296]{1,0:T(8,128)(2,1)S(1)} %stack.13), channel_id=1, source_target_pairs={{0,64},{64,0},{1,65},{65,1},{2,66},{66,2},{3,67},{67,3},{4,68},{68... | collective-permute-start | bytes 4202504 | tf_op jit(solution)/shard_map/ppermute | solution.py:48
  45.1 8.8 %collective-permute-start.11 = (bf16[96,7296]{1,0:T(8,128)(2,1)S(1)}, bf16[96,7296]{1,0:T(8,128)(2,1)S(1)}, u32[]{:S(2)}, u32[]{:S(2)}) collective-permute-start(bf16[96,7296]{1,0:T(8,128)(2,1)S(1)} %stack.12), channel_id=1, source_target_pairs={{0,64},{64,0},{1,65},{65,1},{2,66},{66,2},{3,67},{67,3},{4,68},{68... | collective-permute-start | bytes 4202504 | tf_op jit(solution)/shard_map/ppermute | solution.py:48
  45.6 12.2 %collective-permute-start.10 = (bf16[96,7296]{1,0:T(8,128)(2,1)S(1)}, bf16[96,7296]{1,0:T(8,128)(2,1)S(1)}, u32[]{:S(2)}, u32[]{:S(2)}) collective-permute-start(bf16[96,7296]{1,0:T(8,128)(2,1)S(1)} %get-tuple-element.31.refs_0_), channel_id=1, source_target_pairs={{0,64},{64,0},{1,65},{65,1},{2,66},{66,2},{3,67},{67,3},{4,68},{68... | collective-permute-start | bytes 4202504 | tf_op jit(solution)/shard_map/ppermute | solution.py:48
  50.2 10.3 %collective-permute-start.14 = (bf16[96,7168]{1,0:T(8,128)(2,1)S(1)}, bf16[96,7168]{1,0:T(8,128)(2,1)S(1)}, u32[]{:S(2)}, u32[]{:S(2)}) collective-permute-start(bf16[96,7168]{1,0:T(8,128)(2,1)S(1)} %experts.6.refs_4_), channel_id=1, source_target_pairs={{0,64},{64,0},{1,65},{65,1},{2,66},{66,2},{3,67},{67,3},{4,68},{68... | collective-permute-start | bytes 4128776 | tf_op jit(solution)/shard_map/ppermute | solution.py:48
  50.7 14.1 %collective-permute-start.21 = (bf16[48,7296]{1,0:T(8,128)(2,1)S(1)}, bf16[48,7296]{1,0:T(8,128)(2,1)S(1)}, u32[]{:S(2)}, u32[]{:S(2)}) collective-permute-start(bf16[48,7296]{1,0:T(8,128)(2,1)S(1)} %get-tuple-element.34.refs_0_), channel_id=1, source_target_pairs={{0,3},{1,0},{2,1},{3,2},{4,7},{5,4},{6,5},{7,6},{8,11},{9,8},{10,9... | collective-permute-start | bytes 2101256 | tf_op jit(solution)/shard_map/ppermute | solution.py:44
  53.9 12.3 %collective-permute-start.22 = (bf16[48,7296]{1,0:T(8,128)(2,1)S(1)}, bf16[48,7296]{1,0:T(8,128)(2,1)S(1)}, u32[]{:S(2)}, u32[]{:S(2)}) collective-permute-start(bf16[48,7296]{1,0:T(8,128)(2,1)S(1)} %get-tuple-element.33.refs_1_.refs_3_), channel_id=1, source_target_pairs={{0,1},{1,2},{2,3},{3,0},{4,5},{5,6},{6,7},{7,4},{8,9},{9,10},{10,1... | collective-permute-start | bytes 2101256 | tf_op jit(solution)/shard_map/ppermute | solution.py:44
  55.9 4.9 %collective-permute-start.15 = (bf16[96,7168]{1,0:T(8,128)(2,1)S(1)}, bf16[96,7168]{1,0:T(8,128)(2,1)S(1)}, u32[]{:S(2)}, u32[]{:S(2)}) collective-permute-start(bf16[96,7168]{1,0:T(8,128)(2,1)S(1)} %experts.7.refs_5_), channel_id=1, source_target_pairs={{0,64},{64,0},{1,65},{65,1},{2,66},{66,2},{3,67},{67,3},{4,68},{68... | collective-permute-start | bytes 4128776 | tf_op jit(solution)/shard_map/ppermute | solution.py:48
  60.4 12.1 %collective-permute-start.13 = (bf16[96,7168]{1,0:T(8,128)(2,1)S(1)}, bf16[96,7168]{1,0:T(8,128)(2,1)S(1)}, u32[]{:S(2)}, u32[]{:S(2)}) collective-permute-start(bf16[96,7168]{1,0:T(8,128)(2,1)S(1)} %get-tuple-element.38), channel_id=1, source_target_pairs={{0,64},{64,0},{1,65},{65,1},{2,66},{66,2},{3,67},{67,3},{4,68},{68... | collective-permute-start | bytes 4128776 | tf_op jit(solution)/shard_map/ppermute | solution.py:48
  61.3 19.6 %collective-permute-start.16 = (bf16[96,7168]{1,0:T(8,128)(2,1)S(1)}, bf16[96,7168]{1,0:T(8,128)(2,1)S(1)}, u32[]{:S(2)}, u32[]{:S(2)}) collective-permute-start(bf16[96,7168]{1,0:T(8,128)(2,1)S(1)} %stack.14), channel_id=1, source_target_pairs={{0,1},{1,2},{2,3},{3,0},{4,5},{5,6},{6,7},{7,4},{8,9},{9,10},{10,1... | collective-permute-start | bytes 4128776 | tf_op jit(solution)/shard_map/ppermute | solution.py:44
  61.5 19.5 %collective-permute-start.17 = (bf16[96,7168]{1,0:T(8,128)(2,1)S(1)}, bf16[96,7168]{1,0:T(8,128)(2,1)S(1)}, u32[]{:S(2)}, u32[]{:S(2)}) collective-permute-start(bf16[96,7168]{1,0:T(8,128)(2,1)S(1)} %stack.15), channel_id=1, source_target_pairs={{0,3},{1,0},{2,1},{3,2},{4,7},{5,4},{6,5},{7,6},{8,11},{9,8},{10,9... | collective-permute-start | bytes 4128776 | tf_op jit(solution)/shard_map/ppermute | solution.py:44
  66.2 2.8 %collective-permute-start.23 = (bf16[48,7296]{1,0:T(8,128)(2,1)S(1)}, bf16[48,7296]{1,0:T(8,128)(2,1)S(1)}, u32[]{:S(2)}, u32[]{:S(2)}) collective-permute-start(bf16[48,7296]{1,0:T(8,128)(2,1)S(1)} %get-tuple-element.42.refs_0_), channel_id=1, source_target_pairs={{0,64},{64,0},{1,65},{65,1},{2,66},{66,2},{3,67},{67,3},{4,68},{68... | collective-permute-start | bytes 2101256 | tf_op jit(solution)/shard_map/ppermute | solution.py:48
  67.2 2.8 %collective-permute-start.24 = (bf16[48,7296]{1,0:T(8,128)(2,1)S(1)}, bf16[48,7296]{1,0:T(8,128)(2,1)S(1)}, u32[]{:S(2)}, u32[]{:S(2)}) collective-permute-start(bf16[48,7296]{1,0:T(8,128)(2,1)S(1)} %get-tuple-element.43.refs_1_), channel_id=1, source_target_pairs={{0,64},{64,0},{1,65},{65,1},{2,66},{66,2},{3,67},{67,3},{4,68},{68... | collective-permute-start | bytes 2101256 | tf_op jit(solution)/shard_map/ppermute | solution.py:48
  80.9 2.5 %collective-permute-start.25 = (bf16[48,7168]{1,0:T(8,128)(2,1)S(1)}, bf16[48,7168]{1,0:T(8,128)(2,1)S(1)}, u32[]{:S(2)}, u32[]{:S(2)}) collective-permute-start(bf16[48,7168]{1,0:T(8,128)(2,1)S(1)} %get-tuple-element.48), channel_id=1, source_target_pairs={{0,64},{64,0},{1,65},{65,1},{2,66},{66,2},{3,67},{67,3},{4,68},{68... | collective-permute-start | bytes 2064392 | tf_op jit(solution)/shard_map/ppermute | solution.py:48
  81.7 2.8 %collective-permute-start.26 = (bf16[48,7168]{1,0:T(8,128)(2,1)S(1)}, bf16[48,7168]{1,0:T(8,128)(2,1)S(1)}, u32[]{:S(2)}, u32[]{:S(2)}) collective-permute-start(bf16[48,7168]{1,0:T(8,128)(2,1)S(1)} %get-tuple-element.49), channel_id=1, source_target_pairs={{0,64},{64,0},{1,65},{65,1},{2,66},{66,2},{3,67},{67,3},{4,68},{68... | collective-permute-start | bytes 2064392 | tf_op jit(solution)/shard_map/ppermute | solution.py:48
  84.8 8.9 %collective-permute-start.29 = (bf16[24,7168]{1,0:T(8,128)(2,1)S(1)}, bf16[24,7168]{1,0:T(8,128)(2,1)S(1)}, u32[]{:S(2)}, u32[]{:S(2)}) collective-permute-start(bf16[24,7168]{1,0:T(8,128)(2,1)S(1)} %get-tuple-element.53), channel_id=1, source_target_pairs={{0,32},{1,33},{2,34},{3,35},{4,36},{5,37},{6,38},{7,39},{8,40},{9,... | collective-permute-start | bytes 1032200 | tf_op jit(solution)/shard_map/ppermute | solution.py:44
  86.5 10.7 %collective-permute-start.28 = (bf16[24,7168]{1,0:T(8,128)(2,1)S(1)}, bf16[24,7168]{1,0:T(8,128)(2,1)S(1)}, u32[]{:S(2)}, u32[]{:S(2)}) collective-permute-start(bf16[24,7168]{1,0:T(8,128)(2,1)S(1)} %get-tuple-element.52), channel_id=1, source_target_pairs={{0,48},{1,49},{2,50},{3,51},{4,52},{5,53},{6,54},{7,55},{8,56},{9,... | collective-permute-start | bytes 1032200 | tf_op jit(solution)/shard_map/ppermute | solution.py:44
  87.5 9.8 %collective-permute-start.27 = (bf16[24,7168]{1,0:T(8,128)(2,1)S(1)}, bf16[24,7168]{1,0:T(8,128)(2,1)S(1)}, u32[]{:S(2)}, u32[]{:S(2)}) collective-permute-start(bf16[24,7168]{1,0:T(8,128)(2,1)S(1)} %get-tuple-element.51), channel_id=1, source_target_pairs={{0,16},{1,17},{2,18},{3,19},{4,20},{5,21},{6,22},{7,23},{8,24},{9,... | collective-permute-start | bytes 1032200 | tf_op jit(solution)/shard_map/ppermute | solution.py:44
  88.9 12.2 %collective-permute-start.20 = (bf16[24,7168]{1,0:T(8,128)(2,1)S(1)}, bf16[24,7168]{1,0:T(8,128)(2,1)S(1)}, u32[]{:S(2)}, u32[]{:S(2)}) collective-permute-start(bf16[24,7168]{1,0:T(8,128)(2,1)S(1)} %get-tuple-element.55), channel_id=1, source_target_pairs={{0,32},{1,33},{2,34},{3,35},{4,36},{5,37},{6,38},{7,39},{8,40},{9,... | collective-permute-start | bytes 1032200 | tf_op jit(solution)/shard_map/ppermute | solution.py:44
  90.8 16.5 %collective-permute-start.19 = (bf16[24,7168]{1,0:T(8,128)(2,1)S(1)}, bf16[24,7168]{1,0:T(8,128)(2,1)S(1)}, u32[]{:S(2)}, u32[]{:S(2)}) collective-permute-start(bf16[24,7168]{1,0:T(8,128)(2,1)S(1)} %get-tuple-element.56), channel_id=1, source_target_pairs={{0,48},{1,49},{2,50},{3,51},{4,52},{5,53},{6,54},{7,55},{8,56},{9,... | collective-permute-start | bytes 1032200 | tf_op jit(solution)/shard_map/ppermute | solution.py:44
  93.7 13.6 %collective-permute-start.18 = (bf16[24,7168]{1,0:T(8,128)(2,1)S(1)}, bf16[24,7168]{1,0:T(8,128)(2,1)S(1)}, u32[]{:S(2)}, u32[]{:S(2)}) collective-permute-start(bf16[24,7168]{1,0:T(8,128)(2,1)S(1)} %get-tuple-element.54), channel_id=1, source_target_pairs={{0,16},{1,17},{2,18},{3,19},{4,20},{5,21},{6,22},{7,23},{8,24},{9,... | collective-permute-start | bytes 1032200 | tf_op jit(solution)/shard_map/ppermute | solution.py:44
  97.4 9.9 %collective-permute-start.30 = (bf16[24,7168]{1,0:T(8,128)(2,1)S(1)}, bf16[24,7168]{1,0:T(8,128)(2,1)S(1)}, u32[]{:S(2)}, u32[]{:S(2)}) collective-permute-start(bf16[24,7168]{1,0:T(8,128)(2,1)S(1)} %add_convert_fusion.6), channel_id=1, source_target_pairs={{0,2},{1,3},{2,0},{3,1},{4,6},{5,7},{6,4},{7,5},{8,10},{9,11},{10,... | collective-permute-start | bytes 1032200 | tf_op jit(solution)/shard_map/ppermute | solution.py:44
  107.7 6.4 %collective-permute-start.33 = (bf16[6,7168]{1,0:T(8,128)(2,1)S(1)}, bf16[6,7168]{1,0:T(8,128)(2,1)S(1)}, u32[]{:S(2)}, u32[]{:S(2)}) collective-permute-start(bf16[6,7168]{1,0:T(8,128)(2,1)S(1)} %get-tuple-element.62), channel_id=1, source_target_pairs={{0,8},{1,9},{2,10},{3,11},{4,12},{5,13},{6,14},{7,15},{8,0},{9,1},... | collective-permute-start | bytes 258056 | tf_op jit(solution)/shard_map/ppermute | solution.py:44
  110.3 7.0 %collective-permute-start.32 = (bf16[6,7168]{1,0:T(8,128)(2,1)S(1)}, bf16[6,7168]{1,0:T(8,128)(2,1)S(1)}, u32[]{:S(2)}, u32[]{:S(2)}) collective-permute-start(bf16[6,7168]{1,0:T(8,128)(2,1)S(1)} %get-tuple-element.63), channel_id=1, source_target_pairs={{0,12},{1,13},{2,14},{3,15},{4,0},{5,1},{6,2},{7,3},{8,4},{9,5},{1... | collective-permute-start | bytes 258056 | tf_op jit(solution)/shard_map/ppermute | solution.py:44
  113.3 6.0 %collective-permute-start.31 = (bf16[6,7168]{1,0:T(8,128)(2,1)S(1)}, bf16[6,7168]{1,0:T(8,128)(2,1)S(1)}, u32[]{:S(2)}, u32[]{:S(2)}) collective-permute-start(bf16[6,7168]{1,0:T(8,128)(2,1)S(1)} %get-tuple-element.61), channel_id=1, source_target_pairs={{0,4},{1,5},{2,6},{3,7},{4,8},{5,9},{6,10},{7,11},{8,12},{9,13},{1... | collective-permute-start | bytes 258056 | tf_op jit(solution)/shard_map/ppermute | solution.py:44
